TPU v7x, 128 devices: a whole 4x4x4 slice. The times are simulated.
128 devices in a mesh: expert: 4 (over z_lo, core), hidden: 32 (over x, z_hi, y).
Axes of the slice: x: 4, y: 4, z: 4 (z_hi: 2, z_lo: 2; z = z_hi * 2 + z_lo), core: 2. Of those that a mesh axis runs over, the one named last changes fastest.
Arguments:
- tokens: bfloat16 [1536, 6144], P(('expert', 'hidden')), may hold values from -6 to 6
- routes: int32 [1536, 2], P(('expert', 'hidden')), may hold values from 0 to 3, all different within a row; in each aligned block of 12 rows (0 to 11, 12 to 23, ...) at most 8 rows name the same one
- combine: float32 [1536, 2], P(('expert', 'hidden')), may hold values from 0.25 to 1
- gate_weight: bfloat16 [4, 6144, 16384], P('expert', None, 'hidden'), may hold values from -0.078125 to 0.078125
- up_weight: bfloat16 [4, 6144, 16384], P('expert', None, 'hidden'), may hold values from -0.078125 to 0.078125
- down_weight: bfloat16 [4, 16384, 6144], P('expert', 'hidden'), may hold values from -0.046875 to 0.046875
Outputs:
- mixed: bfloat16 [1536, 6144], P(('expert', 'hidden'))
Inputs may be any that keep to these rules, and one draw needn't show every extreme that they name: `routes`: within each aligned block of 12 tokens, the 2 experts of a token differ and no expert is chosen by more than 8 tokens; in some blocks one expert is chosen by exactly 8 tokens.
All inputs are finite; a program needn't handle non-finite values.
Results may differ from a plain program's by a relative error of at most 0.0049.
Values may be sent and summed in bfloat16 or wider, within the bound.
A program may use at most 192 MiB of HBM per device.

v0:
```python
import jax
import jax.numpy as jnp
from jax import lax
from jax.sharding import PartitionSpec as P

CAP = 8


def on_device(tokens, routes, combine, gate_weight, up_weight, down_weight):
    tok_rows, model_width = tokens.shape
    experts = lax.axis_size("expert")
    row_block = experts * CAP
    flat_routes = routes.reshape(-1)
    chosen = (flat_routes[:, None] == jnp.arange(experts, dtype=jnp.int32)[None, :]).astype(
        jnp.int32
    )
    before = jnp.cumsum(chosen, axis=0) - chosen
    slot_index = jnp.sum(before * chosen, axis=1)
    target = flat_routes * CAP + slot_index
    copies = jnp.repeat(tokens, 2, axis=0)
    outgoing = jnp.zeros((row_block, model_width), tokens.dtype).at[target].set(copies)
    slot_onehot = (slot_index[:, None] == jnp.arange(CAP, dtype=jnp.int32)[None, :]).astype(
        jnp.float32
    )
    weighted = chosen.astype(jnp.float32) * combine.reshape(-1)[:, None]
    combine_table = (
        (weighted[:, :, None] * slot_onehot[:, None, :]).reshape(tok_rows, 2, row_block).sum(axis=1)
    )
    arrived = lax.all_to_all(
        outgoing.reshape(experts, CAP, model_width),
        "expert",
        split_axis=0,
        concat_axis=0,
        tiled=True,
    )
    local_rows = arrived.reshape(row_block, model_width)
    w_gate = gate_weight[0]
    w_up = up_weight[0]
    w_down = down_weight[0]
    rows_part = lax.all_gather(local_rows, "hidden", axis=0, tiled=True)
    gate_out = jnp.dot(rows_part, w_gate, preferred_element_type=jnp.float32)
    up_out = jnp.dot(rows_part, w_up, preferred_element_type=jnp.float32)
    hidden = (jax.nn.silu(gate_out) * up_out).astype(jnp.bfloat16)
    summed = lax.psum_scatter(
        jnp.dot(hidden, w_down, preferred_element_type=jnp.float32),
        "hidden",
        scatter_dimension=0,
        tiled=True,
    )
    returned = lax.all_to_all(
        summed.reshape(experts, CAP, model_width), "expert", split_axis=0, concat_axis=0, tiled=True
    )
    mixed = jnp.dot(
        combine_table,
        returned.reshape(row_block, model_width),
        precision=lax.Precision.HIGHEST,
        preferred_element_type=jnp.float32,
    )
    return mixed.astype(jnp.bfloat16)


def solution(mesh):
    placed = (
        P(("expert", "hidden"), None),
        P(("expert", "hidden"), None),
        P(("expert", "hidden"), None),
        P("expert", None, "hidden"),
        P("expert", None, "hidden"),
        P("expert", "hidden", None),
    )
    return jax.shard_map(
        on_device,
        mesh=mesh,
        in_specs=placed,
        out_specs=P(("expert", "hidden"), None),
        check_vma=False,
    )
```

profile of v0, /device:TPU:1, one launch (start us, length us, event | category | flops | bytes accessed | tf_op | source)
XLA Modules:
  0.0 513.1 jit_solution(13021175758205069907)
XLA Ops:
  6.5 0.0 all-gather.2.cloned.1.call-start
  6.5 0.8 copy.10
  7.3 0.7 broadcast_multiply_fusion.1
  8.0 0.1 eq.36
  8.1 0.1 fusion.11
  8.2 0.2 select_reduce_fusion
  8.4 0.1 copy.12
  8.5 0.1 mul.63
  8.6 1.1 broadcast_in_dim.5
  9.7 0.1 reshape.120
  9.8 1.1 scatter_custom_fusion
  10.9 11.0 %all_to_all.10 = bf16[4,8,6144]{2,1,0:T(8,128)(2,1)} all-to-all(bf16[4,8,6144]{2,1,0:T(8,128)(2,1)S(1)} %bitcast.28), channel_id=1, replica_groups=mesh['expert'=4,'hidden'=32] {'expert'}, dimensions={0} | all-to-all | bytes 786432 | tf_op jit(solution)/shard_map/all_to_all | solution.py:29
  21.9 0.0 all-gather.2.cloned.1.call-update
  21.9 0.0 reduce-scatter.2.cloned.1.call-start
  22.0 132.3 %all-gather.2.cloned.1.call-done = bf16[1024,6144]{1,0:T(8,128)(2,1)} async-done(((bf16[32,6144]{1,0:T(8,128)(2,1)}), bf16[1024,6144]{1,0:T(8,128)(2,1)}) %all-gather.2.cloned.1.call-update) | async-done | bytes 12582928 | tf_op jit(solution)/shard_map/all_gather | solution.py:40
  154.3 0.0 copy-start.1
  154.3 11.6 %fusion.2 = f32[1024,512]{1,0:T(8,128)S(1)} fusion(bf16[1024,6144]{1,0:T(8,128)(2,1)} %all-gather.2.cloned.1.call-done, bf16[1,6144,512]{2,1,0:T(8,128)(2,1)} %param.10), kind=kOutput, calls=%fused_computation.4 | convolution fusion | flops 6442450944 | bytes 20971520 | tf_op jit(solution)/shard_map/dot_general | solution.py:42
  165.9 0.0 copy-done.1
  165.9 8.9 %multiply_convert_fusion = bf16[1024,512]{1,0:T(8,128)(2,1)S(1)} fusion(f32[1024,512]{1,0:T(8,128)S(1)} %fusion.2, bf16[1024,6144]{1,0:T(8,128)(2,1)S(1)} %copy-done.1, bf16[1,6144,512]{2,1,0:T(8,128)(2,1)} %param.9), kind=kOutput, calls=%fused_computation.8 | convolution fusion | flops 6445596672 | bytes 22020096 | tf_op jit(solution)/shard_map/dot_general | solution.py:41
  174.9 14.6 %fusion = f32[1024,6144]{1,0:T(8,128)} fusion(bf16[1024,512]{1,0:T(8,128)(2,1)S(1)} %multiply_convert_fusion, bf16[1,512,6144]{2,1,0:T(8,128)(2,1)} %param.11), kind=kOutput, calls=%fused_computation.2 | convolution fusion | flops 6442450944 | bytes 32505856 | tf_op jit(solution)/shard_map/dot_general | solution.py:45
  189.4 0.0 reduce-scatter.2.cloned.1.call-update
  189.5 0.7 copy-done
  190.1 0.1 copy.11
  190.2 0.1 mul.54
  190.3 297.9 %reduce-scatter.2.cloned.1.call-done = f32[32,6144]{1,0:T(8,128)} async-done(((f32[1024,6144]{1,0:T(8,128)}), f32[32,6144]{1,0:T(8,128)}) %reduce-scatter.2.cloned.1.call-update) | async-done | bytes 786448 | tf_op jit(solution)/shard_map/reduce_scatter | solution.py:44
  488.2 6.1 %all-to-all-start.1 = ((f32[4,8,6144]{2,1,0:T(8,128)}), f32[4,8,6144]{2,1,0:T(8,128)S(1)}, u32[]{:S(2)}, u32[]{:S(2)}) async-start(f32[4,8,6144]{2,1,0:T(8,128)} %bitcast.29), calls=%async_computation.2 | async-start | bytes 1572864 | tf_op jit(solution)/shard_map/all_to_all | solution.py:50
  494.3 0.1 fusion.12
  494.4 0.1 convert_multiply_fusion
  494.4 0.1 broadcast_multiply_fusion
  494.5 0.1 mul.61
  494.7 10.4 %all-to-all-done.1 = f32[4,8,6144]{2,1,0:T(8,128)S(1)} async-done(((f32[4,8,6144]{2,1,0:T(8,128)}), f32[4,8,6144]{2,1,0:T(8,128)S(1)}, u32[]{:S(2)}, u32[]{:S(2)}) %all-to-all-start.1) | async-done | bytes 786464 | tf_op jit(solution)/shard_map/all_to_all | solution.py:50
  505.1 1.2 convolution_convert_fusion
  (4 shorter events, 0.1 us)
Async XLA Ops:
  6.5 147.8 %all-gather.2.cloned.1.call-start = ((), (), s32[]{:S(2)}) async-start(), calls=%async_computation.3 | async-start | bytes 12976128 | tf_op jit(solution)/shard_map/all_gather | solution.py:40
  21.9 466.3 %reduce-scatter.2.cloned.1.call-start = ((), (), s32[]{:S(2)}) async-start(), calls=%async_computation.4 | async-start | bytes 25952256 | tf_op jit(solution)/shard_map/reduce_scatter | solution.py:44
  154.3 11.6 %copy-start.1 = (bf16[1024,6144]{1,0:T(8,128)(2,1)S(1)}, bf16[1024,6144]{1,0:T(8,128)(2,1)}, u32[]{:S(2)}) copy-start(bf16[1024,6144]{1,0:T(8,128)(2,1)} %all-gather.2.cloned.1.call-done) | copy-start | bytes 37748740
  189.4 0.7 copy-start
  488.2 16.9 %all-to-all-start.1 = ((f32[4,8,6144]{2,1,0:T(8,128)}), f32[4,8,6144]{2,1,0:T(8,128)S(1)}, u32[]{:S(2)}, u32[]{:S(2)}) async-start(f32[4,8,6144]{2,1,0:T(8,128)} %bitcast.29), calls=%async_computation.2 | async-start | bytes 1572864 | tf_op jit(solution)/shard_map/all_to_all | solution.py:50
Sparse Core Ops, SparseCore 0:
  22.1 132.2 all-gather.1
  189.6 298.6 reduce-scatter.1
where the time goes:
time: 513 us
  waiting for transfers between devices  441 us (86%)
  matrix products  36.3 us (7%)
  between operations  13.5 us (3%)
  blocking collectives  11 us (2%)
  starting transfers between devices  6.11 us (1%)
    reduce_scatter x1, waiting for transfers between devices, on_device(): lax.psum_scatter(jnp.dot(hidden, w_down, preferred_element_type=jnp.float...  298 us
    all_gather x1, waiting for transfers between devices, on_device(): rows_part = lax.all_gather(local_rows, 'hidden', axis=0, tiled=True)  132 us
    dot_general x1, matrix products, on_device(): jnp.dot(hidden, w_down, preferred_element_type=jnp.float32)  14.6 us
    dot_general x1, matrix products, on_device(): up_out = jnp.dot(rows_part, w_up, preferred_element_type=jnp.float32)  11.6 us
    all_to_all x1, blocking collectives, on_device(): lax.all_to_all(outgoing.reshape(experts, CAP, model_width), 'expert', spl...  11 us
    all_to_all x1, waiting for transfers between devices, on_device(): lax.all_to_all(summed.reshape(experts, CAP, model_width), 'expert', split...  10.4 us
  transfers between devices with their start and end apart: 3, of which 3 were waited for; matrix products, arithmetic and copies ran while one was open for 0% of the time, Pallas kernels for 0%

commit v1 on v0

v1 whole, which is shorter than its diff:
```python
import jax
import jax.numpy as jnp
from jax import lax
from jax.experimental import pallas as pl
from jax.experimental.pallas import tpu as pltpu
from jax.sharding import PartitionSpec as P

MESH = pl.DeviceIdType.MESH
BF16, F32 = jnp.bfloat16, jnp.float32
ROWS = 12
UNIT = 2 * ROWS
PAD = 32
GROUP = 4 * UNIT


def hot(axis):
    if isinstance(axis, int):
        return tuple(int(axis == j) for j in range(3))
    return (lax.div((2 - axis) * (1 - axis), 2), axis * (2 - axis), lax.div(axis * (axis - 1), 2))


class Place:
    def __init__(self):
        e, h = lax.axis_index("expert"), lax.axis_index("hidden")
        self.expert = e
        self.core = lax.rem(e, 2)
        self.at = (
            lax.div(h, 8),
            lax.rem(h, 4),
            lax.rem(lax.div(h, 4), 2) * 2 + lax.div(e, 2),
        )

    def device(self, at, core):
        x, y, z = at
        return {
            "expert": lax.rem(z, 2) * 2 + core,
            "hidden": x * 8 + lax.div(z, 2) * 4 + y,
        }

    def sibling(self):
        return self.device(self.at, 1 - self.core)

    def axis(self, p, k):
        return (p + k) % 3 if isinstance(p, int) else lax.rem(p + k, 3)

    def coord(self, p, k):
        return sum(a * o for a, o in zip(self.at, hot(self.axis(p, k))))

    def along(self, p, k, step):
        on = hot(self.axis(p, k))
        return self.device(tuple(lax.rem(a + step * o, 4) for a, o in zip(self.at, on)), self.core)

    def unit(self, p, i1, i2, i3):
        total = 0
        for k, i in enumerate((i1, i2, i3)):
            o = hot(self.axis(p, k))
            total = total + i * (16 * o[0] + 4 * o[1] + o[2])
        return total


def meet(place):
    barrier = pltpu.get_barrier_semaphore()
    partners = [place.sibling()]
    for a in range(3):
        partners += [place.along(a, 0, 1), place.along(a, 0, 3)]
    for partner in partners:
        pl.semaphore_signal(barrier, inc=1, device_id=partner, device_id_type=MESH)
    pl.semaphore_wait(barrier, len(partners))


def wires(send_sem, recv_sem):
    def wire(slot, src, dst, device):
        return pltpu.make_async_remote_copy(
            src_ref=src,
            dst_ref=dst,
            send_sem=send_sem.at[slot],
            recv_sem=recv_sem.at[slot],
            device_id=device,
            device_id_type=MESH,
        )

    return wire


def each(body):
    pl.loop(0, 3)(body)


def plus(i, n):
    return lax.rem(i + n, 4)


class Gather:
    def __init__(self, place, wire, base, k, pick, parts=1):
        self.place, self.wire, self.base, self.k, self.pick, self.parts = (
            place, wire, base, k, pick, parts,
        )

    slots = 12

    def own(self, p, half, step):
        ref = self.pick(p, half, self.place.coord(p, self.k))
        slot = self.base + (half * 2 + (0 if step == 1 else 1)) * 3 + p
        return self.wire(slot, ref, ref, self.place.along(p, self.k, step))

    def passed(self, p, half, part=0):
        i = plus(self.place.coord(p, self.k), 3 if half == 0 else 1)
        ref = self.pick(p, half, i)
        if self.parts > 1:
            n = ref.shape[0] // self.parts
            ref = ref.at[pl.ds(part * n, n)]
        slot = self.base + 12 + (part * 2 + half) * 3 + p
        return self.wire(slot, ref, ref, self.place.along(p, self.k, 1 if half == 0 else 3))

    def start(self, p):
        self.own(p, 0, 1).start()
        self.own(p, 1, 3).start()
        self.own(p, 1, 1).start()
        self.own(p, 0, 3).start()

    def middle(self, p):
        self.own(p, 0, 1).wait_recv()
        for n in range(self.parts):
            self.passed(p, 0, n).start()
        self.own(p, 1, 3).wait_recv()
        for n in range(self.parts):
            self.passed(p, 1, n).start()

    def near(self, p):
        self.own(p, 1, 1).wait_recv()
        self.own(p, 0, 3).wait_recv()

    def far(self, p):
        for n in range(self.parts):
            self.passed(p, 0, n).wait_recv()
            self.passed(p, 1, n).wait_recv()

    def sent(self, p):
        for half in range(2):
            self.own(p, half, 1).wait_send()
            self.own(p, half, 3).wait_send()
            for n in range(self.parts):
                self.passed(p, half, n).wait_send()


LAST = 4


def gather_kernel(
    t_ref, c_ref, gate_ref, up_ref, out_ref,
    w_ref, other, other_c, first, first_c, x_ref, table, acc, load_sem, send_sem, recv_sem,
):
    place = Place()
    core, sibling = place.core, place.sibling()
    wire = wires(send_sem, recv_sem)
    width = x_ref.shape[-1]
    ff = gate_ref.shape[1]
    part = 4 * width

    loads = [
        pltpu.make_async_copy(gate_ref, w_ref.at[:, pl.ds(0, ff)], load_sem.at[0]),
        pltpu.make_async_copy(up_ref, w_ref.at[:, pl.ds(ff, ff)], load_sem.at[1]),
    ]
    for load in loads:
        load.start()
    meet(place)

    trade = [
        wire(0, t_ref.at[1 - core], other, sibling),
        wire(1, c_ref, other_c, sibling),
    ]
    for t in trade:
        t.start()

    @pl.loop(0, acc.shape[0])
    def _(u):
        acc[u] = jnp.zeros(acc.shape[1:], F32)

    g1 = Gather(place, wire, 2, 0, lambda p, half, i: first.at[p, half, i])
    g2 = Gather(
        place, wire, 20, 1,
        lambda p, half, i: x_ref.at[p, 2 * core + half, place.coord(p, 2), i],
    )
    g3 = Gather(place, wire, 38, 2, lambda p, half, i: x_ref.at[p, 2 * core + half, i], LAST)
    table_base = 38 + 12 + 6 * LAST
    views = (
        lambda i: first_c.at[i],
        lambda i: table.at[place.coord(0, 2), i],
        lambda i: table.at[i],
    )

    def table_wire(k, n):
        me = place.coord(0, k)
        ref = views[k](me if n < 2 else plus(me, 3))
        return wire(table_base + 3 * k + n, ref, ref, place.along(0, k, 3 if n == 1 else 1))

    joined_base = table_base + 9

    def joined(p, i, kind, half=None, part=None):
        if half is None:
            ref = x_ref.at[p, pl.ds(2 * core, 2), i]
        elif part is None:
            ref = x_ref.at[p, 2 * core + half, i]
        else:
            n = 4 // LAST
            ref = x_ref.at[p, 2 * core + half, i, pl.ds(part * n, n)]
        return wire(joined_base + kind * 3 + p, ref, ref, sibling)

    for t in trade:
        t.wait_recv()

    @each
    def _(p):
        for half in range(2):
            first[p, half, place.coord(p, 0)] = t_ref[core, p, half] + other[p, half]
        g1.start(p)

    first_c[place.coord(0, 0)] = c_ref[...] + other_c[...]
    table_wire(0, 0).start()
    table_wire(0, 1).start()
    each(g1.middle)
    table_wire(0, 0).wait_recv()
    table_wire(0, 2).start()

    @each
    def _(p):
        g1.near(p)
        g1.far(p)
        for half in range(2):
            rows = jnp.concatenate(
                [first[p, half, i].astype(F32)[:UNIT] for i in range(4)], axis=0
            )
            x_ref[p, 2 * core + half, place.coord(p, 2), place.coord(p, 1)] = rows.astype(BF16)
        g2.start(p)

    table_wire(0, 1).wait_recv()
    table_wire(0, 2).wait_recv()
    table[place.coord(0, 2), place.coord(0, 1)] = (
        first_c[0] + first_c[1] + first_c[2] + first_c[3]
    )
    table_wire(1, 0).start()
    table_wire(1, 1).start()
    each(g2.middle)
    table_wire(1, 0).wait_recv()
    table_wire(1, 2).start()

    @each
    def _(p):
        g2.near(p)
        g2.far(p)
        g3.start(p)
        joined(p, place.coord(p, 2), 0).start()

    table_wire(1, 1).wait_recv()
    table_wire(1, 2).wait_recv()
    table_wire(2, 0).start()
    table_wire(2, 1).start()

    def gate_up(p, i3):
        @pl.loop(0, w_ref.shape[1] // ff)
        def _(n):
            cols = pl.ds(pl.multiple_of(n * ff, ff), ff)
            rows = jnp.concatenate(
                [x_ref[p, k, i3].reshape(4 * GROUP, width) for k in range(4)], axis=1
            )
            part_rows = pl.ds(pl.multiple_of(p * part, part), part)
            result = jnp.dot(rows, w_ref[part_rows, cols], preferred_element_type=F32)
            for i2 in range(4):
                for i1 in range(4):
                    at = (i2 * 4 + i1) * UNIT
                    u = place.unit(p, i1, i2, i3)
                    acc[u, :, cols] = acc[u, :, cols] + result[at : at + UNIT]

    for load in loads:
        load.wait()

    @each
    def _(p):
        joined(p, place.coord(p, 2), 0).wait_recv()
        gate_up(p, place.coord(p, 2))

    @each
    def _(p):
        me = place.coord(p, 2)
        g3.middle(p)
        joined(p, plus(me, 3), 1, 0).start()
        joined(p, plus(me, 1), 2, 1).start()

    table_wire(2, 0).wait_recv()
    table_wire(2, 2).start()

    @each
    def _(p):
        me = place.coord(p, 2)
        g3.near(p)
        joined(p, plus(me, 3), 3, 1).start()
        joined(p, plus(me, 1), 4, 0).start()

    @each
    def _(p):
        me = place.coord(p, 2)
        joined(p, plus(me, 3), 1, 0).wait_recv()
        joined(p, plus(me, 3), 3, 1).wait_recv()
        gate_up(p, plus(me, 3))

    @each
    def _(p):
        me = place.coord(p, 2)
        joined(p, plus(me, 1), 2, 1).wait_recv()
        joined(p, plus(me, 1), 4, 0).wait_recv()
        gate_up(p, plus(me, 1))

    for n in range(LAST):
        @each
        def _(p):
            me = place.coord(p, 2)
            for half in range(2):
                g3.passed(p, half, n).wait_recv()
                joined(p, plus(me, 2), 5 + 2 * n + half, half, n).start()

    @each
    def _(p):
        me = place.coord(p, 2)
        for n in range(LAST):
            for half in range(2):
                joined(p, plus(me, 2), 5 + 2 * n + half, half, n).wait_recv()
        gate_up(p, plus(me, 2))

    table_wire(2, 1).wait_recv()
    table_wire(2, 2).wait_recv()

    lane = lax.broadcasted_iota(jnp.int32, (UNIT, 128), 1)
    row = lax.broadcasted_iota(jnp.int32, (UNIT, 128), 0)
    token = jnp.where(row < ROWS, row, row - ROWS)
    chosen = lane == token * 4 + place.expert

    @pl.loop(0, 16)
    def _(yz):
        y, z = lax.div(yz, 4), lax.rem(yz, 4)
        own = table[z, y]
        for x in range(4):
            u = x * 16 + yz
            pair = jnp.where(row < ROWS, own[2 * x : 2 * x + 1], own[2 * x + 1 : 2 * x + 2])
            weight = jnp.sum(jnp.where(chosen, pair, 0.0), axis=1, keepdims=True)
            gate, up = acc[u, :, :ff], acc[u, :, ff:]
            out_ref[u, :, :ff] = gate / (1.0 + jnp.exp(-gate)) * up
            out_ref[u, :, ff:] = jnp.broadcast_to(weight, (UNIT, 128))

    for t in trade:
        t.wait_send()
    for k in range(3):
        for n in range(3):
            table_wire(k, n).wait_send()

    @each
    def _(p):
        me = place.coord(p, 2)
        for g in (g1, g2, g3):
            g.sent(p)
        joined(p, me, 0).wait_send()
        joined(p, plus(me, 3), 1, 0).wait_send()
        joined(p, plus(me, 1), 2, 1).wait_send()
        joined(p, plus(me, 3), 3, 1).wait_send()
        joined(p, plus(me, 1), 4, 0).wait_send()
        for n in range(LAST):
            for half in range(2):
                joined(p, plus(me, 2), 5 + 2 * n + half, half, n).wait_send()


GATHER_SLOTS = 38 + 12 + 6 * LAST + 9 + 3 * (5 + 2 * LAST)


class Reduce:
    slots = 18

    def __init__(self, place, wire, base, k, pick, far, plain, merged):
        self.place, self.wire, self.base, self.k, self.pick = place, wire, base, k, pick
        self.far, self.plain, self.merged = far, plain, merged

    def copy(self, p, n, d, half, into, step):
        return self.wire(
            self.base + n * 3 + p, self.pick(p, d, half), into.at[p, half],
            self.place.along(p, self.k, step),
        )

    def opposite(self, p, half):
        return self.copy(p, half, 2, half, self.far, 1 if half == 0 else 3)

    def direct(self, p, half):
        return self.copy(p, 2 + half, 1 if half == 1 else 3, half, self.plain, 1 if half == 1 else 3)

    def relayed(self, p, half):
        return self.copy(p, 4 + half, 1 if half == 0 else 3, half, self.merged, 1 if half == 0 else 3)

    def merge(self, p):
        for half in range(2):
            self.opposite(p, half).wait_recv()
            ref = self.pick(p, 1 if half == 0 else 3, half)
            ref[...] = (ref[...].astype(F32) + self.far[p, half].astype(F32)).astype(BF16)
            self.relayed(p, half).start()

    def total(self, p, half):
        self.direct(p, half).wait_recv()
        self.relayed(p, half).wait_recv()
        return (
            self.pick(p, 0, half)[...].astype(F32)
            + self.plain[p, half].astype(F32)
            + self.merged[p, half].astype(F32)
        )

    def sent(self, p):
        for half in range(2):
            self.opposite(p, half).wait_send()
            self.direct(p, half).wait_send()
            self.relayed(p, half).wait_send()


def reduce_kernel(
    h_ref, down_ref, out_ref,
    w_ref, hp, wp, give, take, own, far1, plain1, merged1,
    z2, far2, plain2, merged2, z3, far3, plain3, merged3, load_sem, send_sem, recv_sem,
):
    place = Place()
    core, sibling = place.core, place.sibling()
    wire = wires(send_sem, recv_sem)
    width = own.shape[-1]
    ff = down_ref.shape[0]

    def load(p, which):
        begin = p * 4 * width + (core if which == 0 else 1 - core) * 2 * width
        return pltpu.make_async_copy(
            down_ref.at[:, pl.ds(pl.multiple_of(begin, 2 * width), 2 * width)],
            w_ref.at[which, p],
            load_sem.at[which * 3 + p],
        )

    for which in (1, 0):
        for p in range(3):
            load(p, which).start()
    meet(place)

    r1 = Reduce(place, wire, 0, 2, lambda p, d, half: own.at[p, d, half], far1, plain1, merged1)
    r2 = Reduce(
        place, wire, 18, 1,
        lambda p, d, half: z2.at[p, half, plus(place.coord(p, 1), d)], far2, plain2, merged2,
    )
    r3 = Reduce(
        place, wire, 36, 0,
        lambda p, d, half: z3.at[p, half, plus(place.coord(p, 0), d)], far3, plain3, merged3,
    )

    def handed(p, d):
        return wire(54 + d * 3 + p, give.at[p, d], take.at[p, d], sibling)

    def product(p, which, half):
        cols = pl.ds(pl.multiple_of(half * width, width), width)
        scale = wp[p]
        return jnp.dot(
            hp[p], w_ref[which, p, :, cols], preferred_element_type=F32
        ) * jnp.concatenate([scale] * (width // 128), axis=1)

    def for_sibling(d):
        @each
        def _(p):
            i3 = plus(place.coord(p, 2), d)
            units = [place.unit(p, i1, i2, i3) for i2 in range(4) for i1 in range(4)]
            for i in range(4):
                rows = [h_ref[u] for u in units[4 * i : 4 * i + 4]]
                at = pl.ds(i * GROUP, GROUP)
                hp[p, at, :] = jnp.concatenate([r[:, :ff] for r in rows], axis=0).astype(BF16)
                wp[p, at, :] = jnp.concatenate([r[:, ff:] for r in rows], axis=0)

            @pl.loop(0, 2)
            def _(half):
                give[p, d, half] = product(p, 1, half).astype(BF16)

            handed(p, d).start()

    def for_chip(d):
        @each
        def _(p):
            handed(p, d).wait_recv()

            @pl.loop(0, 2)
            def _(half):
                total = product(p, 0, half) + take[p, d, half].astype(F32)
                own[p, d, half] = total.astype(BF16)

            if d == 2:
                r1.opposite(p, 0).start()
                r1.opposite(p, 1).start()
            elif d == 1:
                r1.direct(p, 1).start()
            elif d == 3:
                r1.direct(p, 0).start()

    for p in range(3):
        load(p, 1).wait()
    for_sibling(2)
    for p in range(3):
        load(p, 0).wait()
    for_chip(2)
    for d in (1, 3):
        for_sibling(d)
        for_chip(d)
    each(r1.merge)
    for_sibling(0)
    for_chip(0)

    @each
    def _(p):
        for half in range(2):
            total = r1.total(p, half)
            for i in range(4):
                z2[p, half, i] = total[i * GROUP : (i + 1) * GROUP].astype(BF16)
        r2.opposite(p, 0).start()
        r2.opposite(p, 1).start()
        r2.direct(p, 1).start()
        r2.direct(p, 0).start()

    each(r2.merge)

    @each
    def _(p):
        for half in range(2):
            total = r2.total(p, half)
            for i in range(4):
                rows = total[i * UNIT : (i + 1) * UNIT]
                rows = jnp.concatenate([rows, jnp.zeros((PAD - UNIT, width), F32)], axis=0)
                z3[p, half, i] = rows.astype(BF16)
        r3.opposite(p, 0).start()
        r3.opposite(p, 1).start()
        r3.direct(p, 1).start()
        r3.direct(p, 0).start()

    each(r3.merge)

    @each
    def _(p):
        for half in range(2):
            out_ref[core, p, half] = r3.total(p, half).astype(BF16)

    last = wire(66, out_ref.at[core], out_ref.at[core], sibling)
    last.start()

    @each
    def _(p):
        for r in (r1, r2, r3):
            r.sent(p)
        for d in range(4):
            handed(p, d).wait_send()

    last.wait_recv()
    last.wait_send()


REDUCE_SLOTS = 67


def on_device(tokens, routes, combine, gate_weight, up_weight, down_weight):
    width = tokens.shape[1] // 12
    ff = gate_weight.shape[2]
    place = Place()
    core = place.core
    slabs = tokens.reshape(ROWS, 3, 2, 2, width).transpose(2, 1, 3, 0, 4)
    slabs = lax.dynamic_update_slice(
        jnp.zeros((2, 3, 2, PAD, width), BF16), slabs, (0, 0, 0, ROWS * core, 0)
    )
    experts = jnp.arange(4, dtype=jnp.int32)
    dense = jnp.sum(
        jnp.where(routes[:, :, None] == experts, combine[:, :, None], 0.0), axis=1
    ).reshape(1, 4 * ROWS)
    dense = jnp.pad(dense, ((0, 0), (0, 128 - 4 * ROWS)))
    mine = jnp.arange(8, dtype=jnp.int32)[:, None] == 2 * place.at[0] + core
    dense = jnp.where(mine, dense, 0.0)

    vmem = pl.BlockSpec(memory_space=pltpu.VMEM)
    hbm = pl.BlockSpec(memory_space=pl.ANY)
    hidden = pl.pallas_call(
        gather_kernel,
        out_shape=jax.ShapeDtypeStruct((64, UNIT, ff + 128), F32),
        in_specs=[vmem, vmem, hbm, hbm],
        out_specs=vmem,
        scratch_shapes=[
            pltpu.VMEM((12 * width, 2 * ff), BF16),
            pltpu.VMEM((3, 2, PAD, width), BF16),
            pltpu.VMEM((8, 128), F32),
            pltpu.VMEM((3, 2, 4, PAD, width), BF16),
            pltpu.VMEM((4, 8, 128), F32),
            pltpu.VMEM((3, 4, 4, 4, GROUP, width), BF16),
            pltpu.VMEM((4, 4, 8, 128), F32),
            pltpu.VMEM((64, UNIT, 2 * ff), F32),
            pltpu.SemaphoreType.DMA((2,)),
            pltpu.SemaphoreType.DMA((GATHER_SLOTS,)),
            pltpu.SemaphoreType.DMA((GATHER_SLOTS,)),
        ],
        compiler_params=pltpu.CompilerParams(
            collective_id=0, has_side_effects=True, vmem_limit_bytes=60 * 2**20
        ),
    )(slabs, dense, gate_weight[0], up_weight[0])

    def three(*shape):
        return [pltpu.VMEM((3, 2) + shape + (width,), BF16) for _ in range(3)]

    out = pl.pallas_call(
        reduce_kernel,
        out_shape=jax.ShapeDtypeStruct((2, 3, 2, PAD, width), BF16),
        in_specs=[vmem, hbm],
        out_specs=vmem,
        scratch_shapes=[
            pltpu.VMEM((2, 3, ff, 2 * width), BF16),
            pltpu.VMEM((3, 4 * GROUP, ff), BF16),
            pltpu.VMEM((3, 4 * GROUP, 128), F32),
            pltpu.VMEM((3, 4, 2, 4 * GROUP, width), BF16),
            pltpu.VMEM((3, 4, 2, 4 * GROUP, width), BF16),
            pltpu.VMEM((3, 4, 2, 4 * GROUP, width), BF16),
            *three(4 * GROUP),
            pltpu.VMEM((3, 2, 4, GROUP, width), BF16),
            *three(GROUP),
            pltpu.VMEM((3, 2, 4, PAD, width), BF16),
            *three(PAD),
            pltpu.SemaphoreType.DMA((6,)),
            pltpu.SemaphoreType.DMA((REDUCE_SLOTS,)),
            pltpu.SemaphoreType.DMA((REDUCE_SLOTS,)),
        ],
        compiler_params=pltpu.CompilerParams(
            collective_id=1, has_side_effects=True, vmem_limit_bytes=60 * 2**20
        ),
    )(hidden, down_weight[0])
    rows = lax.dynamic_slice(out, (0, 0, 0, ROWS * core, 0), (2, 3, 2, ROWS, width))
    return rows.transpose(3, 1, 0, 2, 4).reshape(ROWS, 12 * width)


def solution(mesh):
    placed = (
        P(("expert", "hidden"), None),
        P(("expert", "hidden"), None),
        P(("expert", "hidden"), None),
        P("expert", None, "hidden"),
        P("expert", None, "hidden"),
        P("expert", "hidden", None),
    )
    return jax.shard_map(
        on_device,
        mesh=mesh,
        in_specs=placed,
        out_specs=P(("expert", "hidden"), None),
        check_vma=False,
    )
```

time: 513 us -> 141 us (0.27)
  waiting for transfers between devices: 441 us -> 0 us
  Pallas kernels: 0 us -> 135 us
  matrix products: 36.3 us -> 0 us
  between operations: 13.5 us -> 0.07 us
  blocking collectives: 11 us -> 0 us
  starting transfers between devices: 6.11 us -> 0 us
    reduce_scatter x1 -> x0, waiting for transfers between devices: 298 us -> none  [on_device(): lax.psum_scatter(jnp.dot(hidden, w_down, preferred_element_type=jnp.float...]
    pallas_call x0 -> x2, Pallas kernels: none -> 135 us  [the longest x1 74 us: on_device(): pl.pallas_call(gather_kernel, out_shape=jax.ShapeDtypeStruct((64, UNIT, f...]
    all_gather x1 -> x0, waiting for transfers between devices: 132 us -> none  [on_device(): rows_part = lax.all_gather(local_rows, 'hidden', axis=0, tiled=True)]
    dot_general x4 -> x0, matrix products: 36.3 us -> none  [the longest x1 14.6 us: on_device(): jnp.dot(hidden, w_down, preferred_element_type=jnp.float32)]
    all_to_all x1 -> x0, blocking collectives: 11 us -> none  [on_device(): lax.all_to_all(outgoing.reshape(experts, CAP, model_width), 'expert', spl...]
    all_to_all x1 -> x0, waiting for transfers between devices: 10.4 us -> none  [on_device(): lax.all_to_all(summed.reshape(experts, CAP, model_width), 'expert', split...]
    all_to_all x1 -> x0, starting transfers between devices: 6.07 us -> none  [on_device(): lax.all_to_all(summed.reshape(experts, CAP, model_width), 'expert', split...]
  transfers between devices with their start and end apart: 3 -> 0, of which waited for: 3 -> 0; matrix products, arithmetic and copies ran while one was open for 0% -> 0% of each run, Pallas kernels for 0% -> 0%
where the time goes in v1:
time: 141 us
  Pallas kernels  135 us (96%)
  local copies, waits for them, and re-layouts  4.56 us (3%)
    pallas_call x1, Pallas kernels, on_device(): pl.pallas_call(gather_kernel, out_shape=jax.ShapeDtypeStruct((64, UNIT, f...  74 us
    pallas_call x1, Pallas kernels, on_device(): pl.pallas_call(reduce_kernel, out_shape=jax.ShapeDtypeStruct((2, 3, 2, PA...  60.8 us

profile of v1, /device:TPU:1, one launch (start us, length us, event | category | flops | bytes accessed | tf_op | source)
XLA Modules:
  0.0 140.8 jit_solution(12309622037924563950)
XLA Ops:
  0.0 0.7 select_reduce_fusion
  0.7 0.1 copy.14
  0.8 0.1 reshape.17
  0.9 0.7 broadcast_select_fusion.c_ref
  1.6 1.0 reshape.16
  2.7 0.6 dynamic_update_slice.3.t_ref
  3.3 0.0 copy-start
  3.3 0.7 copy-done
  4.0 74.0 %shard_map.64.h_ref = f32[64,24,640]{2,1,0:T(8,128)} custom-call(bf16[2,3,2,32,512]{4,3,2,1,0:T(8,128)(2,1)} %copy-done, f32[8,128]{1,0:T(8,128)} %broadcast_select_fusion.c_ref, bf16[6144,512]{1,0:T(8,128)(2,1)} %bitcast.10, bf16[6144,512]{1,0:T(8,128)(2,1)} %bitcast.11), custom_call_target="tpu_custom_call" | custom-call | tf_op jit(solution)/shard_map/pallas_call | solution.py:579
  78.1 60.8 %shard_map.65 = bf16[2,3,2,32,512]{4,3,2,1,0:T(8,128)(2,1)} custom-call(f32[64,24,640]{2,1,0:T(8,128)} %shard_map.64.h_ref, bf16[512,6144]{1,0:T(8,128)(2,1)} %bitcast.12), custom_call_target="tpu_custom_call" | custom-call | tf_op jit(solution)/shard_map/pallas_call | solution.py:605
  138.9 1.0 dynamic-slice_bitcast_fusion
  139.9 0.2 copy.15
  140.1 0.8 reshape.18
  (4 shorter events, 0.1 us)
Async XLA Ops:
  3.3 0.7 copy-start

commit v2 on v0

v2 whole, which is shorter than its diff:
```python
import jax
import jax.numpy as jnp
from jax import lax
from jax.experimental import pallas as pl
from jax.experimental.pallas import tpu as pltpu
from jax.sharding import PartitionSpec as P

MESH = pl.DeviceIdType.MESH
BF16, F32 = jnp.bfloat16, jnp.float32
ROWS = 12
PARTS = 3
SHARE = ROWS // PARTS
UNIT = 2 * SHARE
GROUP = 4 * UNIT
QUARTER = 4 * GROUP


def hot(axis):
    if isinstance(axis, int):
        return tuple(int(axis == j) for j in range(3))
    return (lax.div((2 - axis) * (1 - axis), 2), axis * (2 - axis), lax.div(axis * (axis - 1), 2))


class Place:
    def __init__(self):
        e, h = lax.axis_index("expert"), lax.axis_index("hidden")
        self.expert = e
        self.core = lax.rem(e, 2)
        self.at = (
            lax.div(h, 8),
            lax.rem(h, 4),
            lax.rem(lax.div(h, 4), 2) * 2 + lax.div(e, 2),
        )

    def device(self, at, core):
        x, y, z = at
        return {
            "expert": lax.rem(z, 2) * 2 + core,
            "hidden": x * 8 + lax.div(z, 2) * 4 + y,
        }

    def sibling(self):
        return self.device(self.at, 1 - self.core)

    def axis(self, p, k):
        return (p + k) % 3 if isinstance(p, int) else lax.rem(p + k, 3)

    def coord(self, p, k):
        return sum(a * o for a, o in zip(self.at, hot(self.axis(p, k))))

    def along(self, p, k, step, other=0):
        on = hot(self.axis(p, k))
        core = 1 - self.core if other else self.core
        return self.device(tuple(lax.rem(a + step * o, 4) for a, o in zip(self.at, on)), core)

def meet(place):
    barrier = pltpu.get_barrier_semaphore()
    partners = [place.sibling()] + [
        place.along(a, 0, step, other) for a in range(3) for step in (1, 2, 3) for other in (0, 1)
    ]
    for partner in partners:
        pl.semaphore_signal(barrier, inc=1, device_id=partner, device_id_type=MESH)
    pl.semaphore_wait(barrier, len(partners))


def each(body):
    pl.loop(0, PARTS)(body)


def plus(i, n):
    return lax.rem(i + n, 4)


class Slots:
    def __init__(self):
        self.count = 0

    def take(self, n):
        base = self.count
        self.count += n
        return base


class Gather:
    def __init__(self, place, wire, slots, k, pick, pieces=1):
        self.place, self.wire, self.k, self.pick, self.pieces = place, wire, k, pick, pieces
        self.base = slots.take(12 + 6 * pieces)

    def own(self, p, half, step):
        ref = self.pick(p, half, self.place.coord(p, self.k))
        slot = self.base + (half * 2 + (0 if step == 1 else 1)) * 3 + p
        return self.wire(slot, ref, ref, self.place.along(p, self.k, step))

    def passed(self, p, half, piece=0):
        ref = self.pick(p, half, plus(self.place.coord(p, self.k), 3 if half == 0 else 1))
        if self.pieces > 1:
            n = ref.shape[0] // self.pieces
            ref = ref.at[pl.ds(piece * n, n)]
        slot = self.base + 12 + (piece * 2 + half) * 3 + p
        return self.wire(slot, ref, ref, self.place.along(p, self.k, 1 if half == 0 else 3))

    def start(self, p):
        self.own(p, 0, 1).start()
        self.own(p, 1, 3).start()
        self.own(p, 1, 1).start()
        self.own(p, 0, 3).start()

    def middle(self, p):
        self.own(p, 0, 1).wait_recv()
        for n in range(self.pieces):
            self.passed(p, 0, n).start()
        self.own(p, 1, 3).wait_recv()
        for n in range(self.pieces):
            self.passed(p, 1, n).start()

    def near(self, p):
        self.own(p, 1, 1).wait_recv()
        self.own(p, 0, 3).wait_recv()

    def far(self, p):
        for n in range(self.pieces):
            self.passed(p, 0, n).wait_recv()
            self.passed(p, 1, n).wait_recv()

    def own_sent(self, p):
        for half in range(2):
            self.own(p, half, 1).wait_send()
            self.own(p, half, 3).wait_send()

    def passed_sent(self, p, half):
        for n in range(self.pieces):
            self.passed(p, half, n).wait_send()


PIECES = 4
SLOTS = 400


def kernel(
    t_ref, c_ref, gate_ref, up_ref, down_ref, out_ref,
    w_ref, wd_ref, first, first_c, x_ref, y_ref, h_ref, table, weight,
    far1, plain1, merged1, z2, got2, z3, got3,
    load_sem, send_sem, recv_sem, credit,
):
    place = Place()
    core, sibling = place.core, place.sibling()
    width = x_ref.shape[-1]
    ff = gate_ref.shape[1]
    block = ff // 2
    slots = Slots()

    def wire(slot, src, dst, device):
        return pltpu.make_async_remote_copy(
            src_ref=src,
            dst_ref=dst,
            send_sem=send_sem.at[slot],
            recv_sem=recv_sem.at[slot],
            device_id=device,
            device_id_type=MESH,
        )

    loads = []
    for n in range(2):
        for m, ref in enumerate((gate_ref, up_ref)):
            loads.append(
                pltpu.make_async_copy(
                    ref.at[:, pl.ds(n * block, block)],
                    w_ref.at[:, pl.ds((2 * n + m) * block, block)],
                    load_sem.at[len(loads)],
                )
            )
    for k in range(4):
        loads.append(
            pltpu.make_async_copy(
                down_ref.at[:, pl.ds(k * width, width)], wd_ref.at[k], load_sem.at[len(loads)]
            )
        )
    for load in loads:
        load.start()
    meet(place)

    base1, base_c = slots.take(24), slots.take(8 + 6)
    others = [(s, o) for s in range(4) for o in range(2) if (s, o) != (0, 0)]

    def dealt(p, s, o):
        to = 1 - core if o else core
        return wire(
            base1 + (2 * s + o) * 3 + p, t_ref.at[to, p], first.at[p, 2 * place.coord(p, 0) + core],
            place.along(p, 0, s, o),
        )

    def dealt_table(s, o):
        at = first_c.at[2 * place.coord(0, 0) + core]
        return wire(base_c + 2 * s + o, c_ref, at, place.along(0, 0, s, o))

    def table_wire(k, s):
        at = table.at[place.coord(0, 2)]
        if k == 1:
            at = at.at[place.coord(0, 1)]
        return wire(base_c + 8 + 3 * (k - 1) + s - 1, at, at, place.along(0, k, s))

    g2 = Gather(
        place, wire, slots, 1,
        lambda p, half, i: x_ref.at[p, 2 * core + half, place.coord(p, 2), i],
    )
    g3 = Gather(
        place, wire, slots, 2, lambda p, half, i: x_ref.at[p, 2 * core + half, i], PIECES
    )
    base_j = slots.take(3 * (5 + 2 * PIECES))

    def joined(p, d, kind, half=None, piece=None):
        i = plus(place.coord(p, 2), d)
        if half is None:
            ref = x_ref.at[p, pl.ds(2 * core, 2), i]
        elif piece is None:
            ref = x_ref.at[p, 2 * core + half, i]
        else:
            n = 4 // PIECES
            ref = x_ref.at[p, 2 * core + half, i, pl.ds(piece * n, n)]
        return wire(base_j + kind * 3 + p, ref, ref, sibling)

    def joined_far(p, half, n):
        return joined(p, 2, 5 + 2 * n + half, half, n)

    def region(p, d, k):
        if d == 0:
            return y_ref.at[p, k]
        return x_ref.at[p, k, plus(place.coord(p, 2), d)]

    base_h, base_r = slots.take(24), slots.take(72)

    def handed(p, d, half):
        return wire(
            base_h + (2 * d + half) * 3 + p, region(p, d, half), region(p, d, 2 + half), sibling
        )

    def quarter(p, d, q, half):
        return region(p, d, 2 + half).at[plus(place.coord(p, 1), q)]

    def ring(p, d, n, q, half, into, step):
        return wire(
            base_r + (6 * d + 2 * n + half) * 3 + p, quarter(p, d, q, half), into.at[d, p, half],
            place.along(p, 1, step),
        )

    def opposite(p, d, half):
        return ring(p, d, 0, 2, half, far1, 1 if half == 0 else 3)

    def direct(p, d, half):
        side = 3 if half == 0 else 1
        return ring(p, d, 1, side, half, plain1, side)

    def relayed(p, d, half):
        side = 1 if half == 0 else 3
        return ring(p, d, 2, side, half, merged1, side)

    base_2, base_3, base_o = slots.take(36), slots.take(9), slots.take(1)

    def second(p, d, s):
        src = z2.at[d, p, plus(place.coord(p, 0), s)]
        return wire(
            base_2 + (3 * d + s - 1) * 3 + p, src, got2.at[d, p, s - 1], place.along(p, 0, s)
        )

    def third(p, d):
        return wire(base_3 + 3 * (d - 1) + p, z3.at[d - 1, p], got3.at[d - 1, p], place.along(p, 2, d))

    last = wire(base_o, out_ref.at[core], out_ref.at[core], sibling)
    assert slots.count <= SLOTS

    def gate_up(d, slot):
        @pl.loop(0, 2)
        def _(n):
            rows = jnp.concatenate(
                [
                    jnp.concatenate(
                        [
                            x_ref[p, k, plus(place.coord(p, 2), d)].reshape(QUARTER, width)
                            for k in range(4)
                        ],
                        axis=1,
                    )
                    for p in range(PARTS)
                ],
                axis=0,
            )
            cols = pl.ds(pl.multiple_of(n * ff, ff), ff)
            result = jnp.dot(rows, w_ref[:, cols], preferred_element_type=F32)
            gate, up = result[:, :block], result[:, block:]
            hidden = gate / (1.0 + jnp.exp(-gate)) * up
            h_ref[slot, :, pl.ds(pl.multiple_of(n * block, block), block)] = hidden.astype(BF16)

    def down(d, slot):
        def scaled(k):
            scale = jnp.concatenate(
                [
                    weight[p, plus(place.coord(p, 2), d)].reshape(QUARTER, 128)
                    for p in range(PARTS)
                ],
                axis=0,
            )
            return jnp.dot(h_ref[slot], wd_ref[k], preferred_element_type=F32) * jnp.concatenate(
                [scale] * (width // 128), axis=1
            )

        for half in range(2):
            result = scaled(2 * (1 - core) + half).astype(BF16)
            for p in range(PARTS):
                region(p, d, half)[...] = result[p * QUARTER : (p + 1) * QUARTER].reshape(
                    4, GROUP, width
                )
            if d and half == 0:
                pl.semaphore_wait(credit.at[d], 1)
            for p in range(PARTS):
                handed(p, d, half).start()
        for half in range(2):
            result = scaled(2 * core + half)
            for p in range(PARTS):
                handed(p, d, half).wait_recv()
                ref = region(p, d, 2 + half)
                mine = result[p * QUARTER : (p + 1) * QUARTER].reshape(4, GROUP, width)
                ref[...] = (mine + ref[...].astype(F32)).astype(BF16)
                opposite(p, d, half).start()
                direct(p, d, half).start()

    def free(d):
        pl.semaphore_signal(credit.at[d], inc=1, device_id=sibling, device_id_type=MESH)

    def merge(d):
        @each
        def _(p):
            for half in range(2):
                opposite(p, d, half).wait_recv()
                ref = quarter(p, d, 1 if half == 0 else 3, half)
                ref[...] = (ref[...].astype(F32) + far1[d, p, half].astype(F32)).astype(BF16)
                relayed(p, d, half).start()

    def total(d):
        @each
        def _(p):
            sums = []
            for half in range(2):
                direct(p, d, half).wait_recv()
                relayed(p, d, half).wait_recv()
                sums.append(
                    quarter(p, d, 0, half)[...].astype(F32)
                    + plain1[d, p, half].astype(F32)
                    + merged1[d, p, half].astype(F32)
                )
            for i in range(4):
                rows = [t[i * UNIT : (i + 1) * UNIT] for t in sums]
                z2[d, p, i] = jnp.concatenate(rows, axis=0).astype(BF16)
            for s in (2, 1, 3):
                second(p, d, s).start()

    def chip_sum(p, d):
        result = z2[d, p, place.coord(p, 0)].astype(F32)
        for s in (1, 2, 3):
            second(p, d, s).wait_recv()
            result = result + got2[d, p, s - 1].astype(F32)
        return result

    for s, o in others:
        for p in range(PARTS):
            dealt(p, s, o).start()
        dealt_table(s, o).start()
    for p in range(PARTS):
        first[p, 2 * place.coord(p, 0) + core] = t_ref[core, p]
    first_c[2 * place.coord(0, 0) + core] = c_ref[...]
    for p in range(PARTS):
        for s, o in others:
            dealt(p, s, o).wait_recv()
        halves = ([], [])
        for i in range(4):
            a, b = first[p, 2 * i].astype(F32), first[p, 2 * i + 1].astype(F32)
            for half in range(2):
                at = half * SHARE
                halves[half].extend([a[at : at + SHARE], b[at : at + SHARE]])
        for half in range(2):
            x_ref[p, 2 * core + half, place.coord(p, 2), place.coord(p, 1)] = jnp.concatenate(
                halves[half], axis=0
            ).astype(BF16)
        g2.start(p)

    for s, o in others:
        dealt_table(s, o).wait_recv()
    table[place.coord(0, 2), place.coord(0, 1)] = sum(first_c[i] for i in range(8))
    for s in (1, 2, 3):
        table_wire(1, s).start()
    each(g2.middle)

    @each
    def _(p):
        g2.near(p)
        g2.far(p)
        g3.start(p)
        joined(p, 0, 0).start()

    for s in (1, 2, 3):
        table_wire(1, s).wait_recv()
    for s in (1, 2, 3):
        table_wire(2, s).start()
    for load in loads[:4]:
        load.wait()
    for p in range(PARTS):
        joined(p, 0, 0).wait_recv()
    gate_up(0, 0)

    @each
    def _(p):
        g3.middle(p)
        joined(p, 3, 1, 0).start()
        joined(p, 1, 2, 1).start()

    for s in (1, 2, 3):
        table_wire(2, s).wait_recv()
    lane = lax.broadcasted_iota(jnp.int32, (UNIT, 128), 1)
    row = lax.broadcasted_iota(jnp.int32, (UNIT, 128), 0)
    token = jnp.where(row < SHARE, row, row - SHARE)

    @pl.loop(0, 16)
    def _(yz):
        y, z = lax.div(yz, 4), lax.rem(yz, 4)
        rows = table[z, y]
        for x in range(4):
            pair = jnp.where(row < SHARE, rows[2 * x : 2 * x + 1], rows[2 * x + 1 : 2 * x + 2])
            at = (x, y, z)
            for p in range(PARTS):
                chosen = lane == (token + p * SHARE) * 4 + place.expert
                value = jnp.sum(jnp.where(chosen, pair, 0.0), axis=1, keepdims=True)
                weight[p, at[(p + 2) % 3], at[(p + 1) % 3], at[p]] = jnp.broadcast_to(
                    value, (UNIT, 128)
                )

    for load in loads[4:]:
        load.wait()
    down(0, 0)

    @each
    def _(p):
        g3.near(p)
        joined(p, 3, 3, 1).start()
        joined(p, 1, 4, 0).start()

    for p in range(PARTS):
        joined(p, 3, 1, 0).wait_recv()
        joined(p, 3, 3, 1).wait_recv()
    gate_up(3, 0)
    merge(0)
    for p in range(PARTS):
        joined(p, 1, 2, 1).wait_recv()
        joined(p, 1, 4, 0).wait_recv()
    gate_up(1, 1)

    @each
    def _(p):
        g3.passed_sent(p, 0)
        joined(p, 3, 1, 0).wait_send()
        joined(p, 3, 3, 1).wait_send()

    free(3)
    down(3, 0)

    @each
    def _(p):
        for n in range(PIECES):
            for half in range(2):
                g3.passed(p, half, n).wait_recv()
                joined_far(p, half, n).start()
        g3.passed_sent(p, 1)
        joined(p, 1, 2, 1).wait_send()
        joined(p, 1, 4, 0).wait_send()

    free(1)
    down(1, 1)
    merge(3)

    @each
    def _(p):
        for n in range(PIECES):
            for half in range(2):
                joined_far(p, half, n).wait_recv()

    gate_up(2, 0)

    @each
    def _(p):
        for n in range(PIECES):
            for half in range(2):
                joined_far(p, half, n).wait_send()

    free(2)
    merge(1)
    total(0)
    down(2, 0)
    total(3)
    merge(2)
    total(1)

    def finish(d):
        @each
        def _(p):
            z3[d - 1, p] = chip_sum(p, d).astype(BF16)
            third(p, d).start()

    finish(3)
    finish(1)
    total(2)
    finish(2)

    @each
    def _(p):
        result = chip_sum(p, 0)
        for d in (3, 1, 2):
            third(p, d).wait_recv()
            result = result + got3[d - 1, p].astype(F32)
        out_ref[core, p] = result.astype(BF16)

    last.start()

    for s, o in others:
        dealt_table(s, o).wait_send()
    for k in (1, 2):
        for s in (1, 2, 3):
            table_wire(k, s).wait_send()

    @each
    def _(p):
        for s, o in others:
            dealt(p, s, o).wait_send()
        g2.own_sent(p)
        g2.passed_sent(p, 0)
        g2.passed_sent(p, 1)
        g3.own_sent(p)
        joined(p, 0, 0).wait_send()
        for d in range(4):
            for half in range(2):
                handed(p, d, half).wait_send()
                opposite(p, d, half).wait_send()
                direct(p, d, half).wait_send()
                relayed(p, d, half).wait_send()
            for s in (1, 2, 3):
                second(p, d, s).wait_send()
            if d:
                third(p, d).wait_send()

    last.wait_recv()
    last.wait_send()


def on_device(tokens, routes, combine, gate_weight, up_weight, down_weight):
    model_width = tokens.shape[1]
    width = model_width // 4
    ff = gate_weight.shape[2]
    place = Place()
    core = place.core
    shares = (
        tokens.reshape(PARTS, SHARE, 2, 2, width)
        .transpose(2, 0, 3, 1, 4)
        .reshape(2, PARTS, 2 * SHARE, width)
    )
    experts = jnp.arange(4, dtype=jnp.int32)
    dense = jnp.sum(
        jnp.where(routes[:, :, None] == experts, combine[:, :, None], 0.0), axis=1
    ).reshape(1, 4 * ROWS)
    dense = jnp.pad(dense, ((0, 0), (0, 128 - 4 * ROWS)))
    mine = jnp.arange(8, dtype=jnp.int32)[:, None] == 2 * place.at[0] + core
    dense = jnp.where(mine, dense, 0.0)

    vmem = pl.BlockSpec(memory_space=pltpu.VMEM)
    hbm = pl.BlockSpec(memory_space=pl.ANY)

    def ring_buffer():
        return pltpu.VMEM((4, PARTS, 2, GROUP, width), BF16)

    out = pl.pallas_call(
        kernel,
        out_shape=jax.ShapeDtypeStruct((2, PARTS, 2 * UNIT, width), BF16),
        in_specs=[vmem, vmem, hbm, hbm, hbm],
        out_specs=vmem,
        scratch_shapes=[
            pltpu.VMEM((model_width, 2 * ff), BF16),
            pltpu.VMEM((4, ff, width), BF16),
            pltpu.VMEM((PARTS, 8, 2 * SHARE, width), BF16),
            pltpu.VMEM((8, 8, 128), F32),
            pltpu.VMEM((PARTS, 4, 4, 4, GROUP, width), BF16),
            pltpu.VMEM((PARTS, 4, 4, GROUP, width), BF16),
            pltpu.VMEM((2, PARTS * QUARTER, ff), BF16),
            pltpu.VMEM((4, 4, 8, 128), F32),
            pltpu.VMEM((PARTS, 4, 4, 4, UNIT, 128), F32),
            ring_buffer(),
            ring_buffer(),
            ring_buffer(),
            pltpu.VMEM((4, PARTS, 4, 2 * UNIT, width), BF16),
            pltpu.VMEM((4, PARTS, 3, 2 * UNIT, width), BF16),
            pltpu.VMEM((3, PARTS, 2 * UNIT, width), BF16),
            pltpu.VMEM((3, PARTS, 2 * UNIT, width), BF16),
            pltpu.SemaphoreType.DMA((8,)),
            pltpu.SemaphoreType.DMA((SLOTS,)),
            pltpu.SemaphoreType.DMA((SLOTS,)),
            pltpu.SemaphoreType.REGULAR((4,)),
        ],
        compiler_params=pltpu.CompilerParams(
            collective_id=0, has_side_effects=True, vmem_limit_bytes=62 * 2**20
        ),
    )(shares, dense, gate_weight[0], up_weight[0], down_weight[0])
    rows = out.reshape(2, PARTS, 2, 2, SHARE, width)
    rows = lax.dynamic_index_in_dim(rows, core, axis=3, keepdims=False)
    return rows.transpose(1, 3, 0, 2, 4).reshape(ROWS, model_width)


def solution(mesh):
    placed = (
        P(("expert", "hidden"), None),
        P(("expert", "hidden"), None),
        P(("expert", "hidden"), None),
        P("expert", None, "hidden"),
        P("expert", None, "hidden"),
        P("expert", "hidden", None),
    )
    return jax.shard_map(
        on_device,
        mesh=mesh,
        in_specs=placed,
        out_specs=P(("expert", "hidden"), None),
        check_vma=False,
    )
```

time: 513 us -> 126 us (0.25)
  waiting for transfers between devices: 441 us -> 0 us
  Pallas kernels: 0 us -> 121 us
  matrix products: 36.3 us -> 0 us
  between operations: 13.5 us -> 0.05 us
  blocking collectives: 11 us -> 0 us
  starting transfers between devices: 6.11 us -> 0 us
    reduce_scatter x1 -> x0, waiting for transfers between devices: 298 us -> none  [on_device(): lax.psum_scatter(jnp.dot(hidden, w_down, preferred_element_type=jnp.float...]
    all_gather x1 -> x0, waiting for transfers between devices: 132 us -> none  [on_device(): rows_part = lax.all_gather(local_rows, 'hidden', axis=0, tiled=True)]
    pallas_call x0 -> x1, Pallas kernels: none -> 121 us  [on_device(): pl.pallas_call(kernel, out_shape=jax.ShapeDtypeStruct((2, PARTS, 2 * UNIT...]
    dot_general x4 -> x0, matrix products: 36.3 us -> none  [the longest x1 14.6 us: on_device(): jnp.dot(hidden, w_down, preferred_element_type=jnp.float32)]
    all_to_all x1 -> x0, blocking collectives: 11 us -> none  [on_device(): lax.all_to_all(outgoing.reshape(experts, CAP, model_width), 'expert', spl...]
    all_to_all x1 -> x0, waiting for transfers between devices: 10.4 us -> none  [on_device(): lax.all_to_all(summed.reshape(experts, CAP, model_width), 'expert', split...]
    all_to_all x1 -> x0, starting transfers between devices: 6.07 us -> none  [on_device(): lax.all_to_all(summed.reshape(experts, CAP, model_width), 'expert', split...]
  transfers between devices with their start and end apart: 3 -> 0, of which waited for: 3 -> 0; matrix products, arithmetic and copies ran while one was open for 0% -> 0% of each run, Pallas kernels for 0% -> 0%
where the time goes in v2:
time: 126 us
  Pallas kernels  121 us (96%)
  local copies, waits for them, and re-layouts  3.93 us (3%)
  other arithmetic  1.38 us (1%)
    pallas_call x1, Pallas kernels, on_device(): pl.pallas_call(kernel, out_shape=jax.ShapeDtypeStruct((2, PARTS, 2 * UNIT...  121 us

profile of v2, /device:TPU:1, one launch (start us, length us, event | category | flops | bytes accessed | tf_op | source)
XLA Modules:
  0.0 126.2 jit_solution(13251833330029234866)
XLA Ops:
  0.0 0.7 select_reduce_fusion
  0.7 0.1 copy.20
  0.8 0.1 reshape.24
  0.9 0.7 broadcast_select_fusion.c_ref
  1.6 1.0 reshape.22
  2.6 0.1 copy.25
  2.7 0.7 reshape.23.t_ref
  3.4 120.8 %shard_map.64 = bf16[2,3,16,1536]{3,2,1,0:T(8,128)(2,1)} custom-call(bf16[2,3,8,1536]{3,2,1,0:T(8,128)(2,1)} %reshape.23.t_ref, f32[8,128]{1,0:T(8,128)} %broadcast_select_fusion.c_ref, bf16[6144,512]{1,0:T(8,128)(2,1)} %bitcast.16, bf16[6144,512]{1,0:T(8,128)(2,1)} %bitcast.17, bf16[512,6144]{1,0:T(8,128)(2,1)} %bitcast.18), custom_call_target="tpu_custom_call" | custom-call | tf_op jit(solution)/shard_map/pallas_call | solution.py:576
  124.2 1.0 reshape.25
  125.2 0.1 dynamic-slice_bitcast_fusion
  125.3 0.1 copy.22
  125.4 0.8 reshape.26
  (2 shorter events, 0.0 us)

commit v3 on v2

v3 whole, which is shorter than its diff:
```python
import jax
import jax.numpy as jnp
from jax import lax
from jax.experimental import pallas as pl
from jax.experimental.pallas import tpu as pltpu
from jax.sharding import PartitionSpec as P

MESH = pl.DeviceIdType.MESH
BF16, F32 = jnp.bfloat16, jnp.float32
ROWS = 12
PARTS = 3
SHARE = ROWS // PARTS
UNIT = 2 * SHARE
GROUP = 4 * UNIT
QUARTER = 4 * GROUP


def hot(axis):
    if isinstance(axis, int):
        return tuple(int(axis == j) for j in range(3))
    return (lax.div((2 - axis) * (1 - axis), 2), axis * (2 - axis), lax.div(axis * (axis - 1), 2))


class Place:
    def __init__(self):
        e, h = lax.axis_index("expert"), lax.axis_index("hidden")
        self.expert = e
        self.core = lax.rem(e, 2)
        self.at = (
            lax.div(h, 8),
            lax.rem(h, 4),
            lax.rem(lax.div(h, 4), 2) * 2 + lax.div(e, 2),
        )

    def device(self, at, core):
        x, y, z = at
        return {
            "expert": lax.rem(z, 2) * 2 + core,
            "hidden": x * 8 + lax.div(z, 2) * 4 + y,
        }

    def sibling(self):
        return self.device(self.at, 1 - self.core)

    def axis(self, p, k):
        return (p + k) % 3 if isinstance(p, int) else lax.rem(p + k, 3)

    def coord(self, p, k):
        return sum(a * o for a, o in zip(self.at, hot(self.axis(p, k))))

    def along(self, p, k, step, other=0):
        on = hot(self.axis(p, k))
        core = 1 - self.core if other else self.core
        return self.device(tuple(lax.rem(a + step * o, 4) for a, o in zip(self.at, on)), core)

def meet(place):
    barrier = pltpu.get_barrier_semaphore()
    partners = [place.sibling()] + [
        place.along(a, 0, step, other) for a in range(3) for step in (1, 2, 3) for other in (0, 1)
    ]
    for partner in partners:
        pl.semaphore_signal(barrier, inc=1, device_id=partner, device_id_type=MESH)
    pl.semaphore_wait(barrier, len(partners))


def each(body):
    pl.loop(0, PARTS)(body)


def plus(i, n):
    return lax.rem(i + n, 4)


class Slots:
    def __init__(self):
        self.count = 0

    def take(self, n):
        base = self.count
        self.count += n
        return base


SENDS, RECVS = 24, 96


def kernel(
    tok_ref, route_ref, comb_ref, gate_ref, up_ref, down_ref, out_ref,
    w_ref, wd_ref, t_ref, c_ref, pad_c, pad_r, first, first_c, x_ref, y_ref, h_ref, table, weight,
    far1, plain1, merged1, z2, got2, z3, got3, o_ref,
    load_sem, send_sem, recv_sem, credit,
):
    place = Place()
    core, sibling = place.core, place.sibling()
    width = x_ref.shape[-1]
    ff = gate_ref.shape[1]
    block = ff // 2
    sends, recvs = Slots(), Slots()

    def wire(send, recv, src, dst, device):
        return pltpu.make_async_remote_copy(
            src_ref=src,
            dst_ref=dst,
            send_sem=send_sem.at[send],
            recv_sem=recv_sem.at[recv],
            device_id=device,
            device_id_type=MESH,
        )

    def sent(slot, ref):
        wire(slot, 0, ref, ref, sibling).wait_send()

    def arrived(slot, ref):
        wire(0, slot, ref, ref, sibling).wait_recv()

    loads = []
    for n in range(2):
        for m, ref in enumerate((gate_ref, up_ref)):
            loads.append(
                pltpu.make_async_copy(
                    ref.at[:, pl.ds(n * block, block)],
                    w_ref.at[:, pl.ds((2 * n + m) * block, block)],
                    load_sem.at[len(loads)],
                )
            )
    for k in range(4):
        loads.append(
            pltpu.make_async_copy(
                down_ref.at[:, pl.ds(k * width, width)], wd_ref.at[k], load_sem.at[len(loads)]
            )
        )

    for k in range(4):
        rows = tok_ref[:, k * width : (k + 1) * width].astype(F32)
        for p in range(PARTS):
            at = (k % 2) * SHARE
            t_ref[k // 2, p, at : at + SHARE] = rows[p * SHARE : (p + 1) * SHARE].astype(BF16)
    pad_c[...] = jnp.zeros(pad_c.shape, F32)
    pad_r[...] = jnp.zeros(pad_r.shape, jnp.int32)
    pad_c[0:2, 0:ROWS] = comb_ref[...]
    pad_r[0:2, 0:ROWS] = route_ref[...]
    spread = pad_c[...] * 0.0
    for e in range(4):
        mine = jnp.where(pad_r[...] == e, pad_c[...], 0.0)
        spread = spread + (pltpu.roll(mine, 16 * e, 1) if e else mine)
    c_ref[...] = jnp.broadcast_to(jnp.sum(spread, axis=0, keepdims=True), (8, 128))

    meet(place)

    others = [(s, o) for s in (0, 1, 3, 2) for o in range(2) if (s, o) != (0, 0)]
    s_deal, r_deal = sends.take(1), recvs.take(3)
    s_table, r_table = sends.take(3), recvs.take(3)

    def dealt(p, s, o):
        to = 1 - core if o else core
        return wire(
            s_deal, r_deal + p, t_ref.at[to, p], first.at[p, 2 * ((4 - s) % 4) + core],
            place.along(p, 0, s, o),
        )

    def dealt_table(s, o):
        at = first_c.at[2 * ((4 - s) % 4) + core]
        return wire(s_table, r_table, c_ref, at, place.along(0, 0, s, o))

    def table_wire(k, s):
        if k == 1:
            src, dst = table.at[0, 0], table.at[0, 4 - s]
        else:
            src, dst = table.at[0], table.at[4 - s]
        return wire(s_table + k, r_table + k, src, dst, place.along(0, k, s))

    s_two, r_two = sends.take(2), recvs.take(9)

    def two(p, half, step):
        at = x_ref.at[p, 2 * core + half, 0]
        kind = 0 if half == (0 if step == 1 else 1) else 2
        slot = r_two + (half if kind == 0 else 2) * 3 + p
        return wire(s_two, slot, at.at[0], at.at[4 - step], place.along(p, 1, step))

    def two_on(p, half):
        at = x_ref.at[p, 2 * core + half, 0]
        step = 1 if half == 0 else 3
        return wire(s_two + 1, r_two + 6 + p, at.at[4 - step], at.at[2], place.along(p, 1, step))

    s_three, r_three = sends.take(3), recvs.take(9 + 12)

    def three(p, half, step, rest):
        at = x_ref.at[p, 2 * core + half]
        groups = pl.ds(1, 3) if rest else pl.ds(0, 1)
        kind = half if half == (0 if step == 1 else 1) else 2
        return wire(
            s_three, r_three + kind * 3 + p, at.at[0, groups], at.at[4 - step, groups],
            place.along(p, 2, step),
        )

    def three_all(p, rest):
        for half, step in ((0, 1), (1, 3), (1, 1), (0, 3)):
            three(p, half, step, rest).start()

    def three_on(p, half, g):
        at = x_ref.at[p, 2 * core + half]
        step = 1 if half == 0 else 3
        return wire(
            s_three + 1 + half, r_three + 9 + 3 * g + p, at.at[4 - step, g], at.at[2, g],
            place.along(p, 2, step),
        )

    s_join, r_join = sends.take(4), recvs.take(4)

    def joined(p, d, half=None, g=None):
        if half is None:
            ref = x_ref.at[p, pl.ds(2 * core, 2), d]
        else:
            ref = x_ref.at[p, 2 * core + half, d]
        if g is not None:
            ref = ref.at[g]
        return wire(s_join + d, r_join + d, ref, ref, sibling)

    half_of_quarter = x_ref.at[:, pl.ds(0, 2), 0]

    def region(p, d, k):
        if d == 0:
            return y_ref.at[p, k]
        return x_ref.at[p, k, {3: 0, 1: 3, 2: 1}[d]]

    s_hand, r_hand = sends.take(1), recvs.take(8)

    def handed(p, d, half):
        return wire(
            s_hand, r_hand + 2 * d + half, region(p, d, half), region(p, d, 2 + half), sibling
        )

    s_ring, r_ring = sends.take(3), recvs.take(24)

    def ring(p, d, n, q, half, into, step):
        slot = r_ring + 3 * d + p + (12 if n else 0)
        return wire(
            s_ring + n, slot, region(p, d, 2 + half).at[q], into.at[d, p, half],
            place.along(p, 1, step),
        )

    def opposite(p, d, half):
        return ring(p, d, 0, 2, half, far1, 1 if half == 0 else 3)

    def direct(p, d, half):
        side = 3 if half == 0 else 1
        return ring(p, d, 1, side, half, plain1, side)

    def relayed(p, d, half):
        side = 1 if half == 0 else 3
        return ring(p, d, 2, side, half, merged1, side)

    s_second, r_second = sends.take(1), recvs.take(12)
    s_third, r_third = sends.take(1), recvs.take(3)
    s_last, r_last = sends.take(1), recvs.take(1)
    assert sends.count <= SENDS and recvs.count <= RECVS

    def second(p, d, s):
        return wire(
            s_second, r_second + 3 * d + p, z2.at[d, p, s], got2.at[d, p, s - 1],
            place.along(p, 0, s),
        )

    def third(p, d):
        return wire(
            s_third, r_third + p, z3.at[d - 1, p], got3.at[d - 1, p], place.along(p, 2, d)
        )

    last = wire(s_last, r_last, o_ref.at[core], o_ref.at[core], sibling)

    def gate_up(d):
        @pl.loop(0, 2)
        def _(n):
            rows = jnp.concatenate(
                [
                    jnp.concatenate(
                        [x_ref[p, k, d].reshape(QUARTER, width) for k in range(4)], axis=1
                    )
                    for p in range(PARTS)
                ],
                axis=0,
            )
            cols = pl.ds(pl.multiple_of(n * ff, ff), ff)
            result = jnp.dot(rows, w_ref[:, cols], preferred_element_type=F32)
            gate, up = result[:, :block], result[:, block:]
            hidden = gate / (1.0 + jnp.exp(-gate)) * up
            h_ref[:, pl.ds(pl.multiple_of(n * block, block), block)] = hidden.astype(BF16)

    def down(d):
        def scaled(k):
            scale = jnp.concatenate(
                [weight[p, d].reshape(QUARTER, 128) for p in range(PARTS)], axis=0
            )
            return jnp.dot(h_ref[...], wd_ref[k], preferred_element_type=F32) * jnp.concatenate(
                [scale] * (width // 128), axis=1
            )

        for half in range(2):
            result = scaled(2 * (1 - core) + half).astype(BF16)
            for p in range(PARTS):
                region(p, d, half)[...] = result[p * QUARTER : (p + 1) * QUARTER].reshape(
                    4, GROUP, width
                )
            if d and half == 0:
                pl.semaphore_wait(credit.at[d], 1)
            for p in range(PARTS):
                handed(p, d, half).start()
        for half in range(2):
            result = scaled(2 * core + half)
            arrived(r_hand + 2 * d + half, x_ref.at[0, pl.ds(0, 3), 0])
            for p in range(PARTS):
                ref = region(p, d, 2 + half)
                mine = result[p * QUARTER : (p + 1) * QUARTER].reshape(4, GROUP, width)
                ref[...] = (mine + ref[...].astype(F32)).astype(BF16)
                opposite(p, d, half).start()
                direct(p, d, half).start()

    def free(d):
        pl.semaphore_signal(credit.at[d], inc=1, device_id=sibling, device_id_type=MESH)

    def merge(d):
        @each
        def _(p):
            arrived(r_ring + 3 * d + p, far1.at[d, p])
            for half in range(2):
                ref = region(p, d, 2 + half).at[1 if half == 0 else 3]
                ref[...] = (ref[...].astype(F32) + far1[d, p, half].astype(F32)).astype(BF16)
                relayed(p, d, half).start()

    def total(d):
        @each
        def _(p):
            arrived(r_ring + 12 + 3 * d + p, x_ref.at[0, 0, 0])
            sums = [
                region(p, d, 2 + half)[0].astype(F32)
                + plain1[d, p, half].astype(F32)
                + merged1[d, p, half].astype(F32)
                for half in range(2)
            ]
            for i in range(4):
                rows = [t[i * UNIT : (i + 1) * UNIT] for t in sums]
                z2[d, p, i] = jnp.concatenate(rows, axis=0).astype(BF16)
            for s in (2, 1, 3):
                second(p, d, s).start()

    def chip_sum(p, d):
        arrived(r_second + 3 * d + p, got2.at[d, p])
        result = z2[d, p, 0].astype(F32)
        for s in (1, 2, 3):
            result = result + got2[d, p, s - 1].astype(F32)
        return result

    for s, o in others:
        for p in range(PARTS):
            dealt(p, s, o).start()
    for s, o in others:
        dealt_table(s, o).start()
    for load in loads:
        load.start()
    for p in range(PARTS):
        first[p, core] = t_ref[core, p]
    first_c[core] = c_ref[...]
    for p in range(PARTS):
        arrived(r_deal + p, first.at[p, pl.ds(0, 7)])
        halves = ([], [])
        for i in range(4):
            a, b = first[p, 2 * i].astype(F32), first[p, 2 * i + 1].astype(F32)
            for half in range(2):
                at = half * SHARE
                halves[half].extend([a[at : at + SHARE], b[at : at + SHARE]])
        for half in range(2):
            x_ref[p, 2 * core + half, 0, 0] = jnp.concatenate(halves[half], axis=0).astype(BF16)
        for half, step in ((0, 1), (1, 3), (1, 1), (0, 3)):
            two(p, half, step).start()
        three_all(p, False)

    arrived(r_table, first_c.at[pl.ds(0, 7)])
    row8 = lax.broadcasted_iota(jnp.int32, (8, 128), 0)
    table[0, 0] = sum(jnp.where(row8 == i, first_c[i], 0.0) for i in range(8))
    for s in (1, 2, 3):
        table_wire(1, s).start()

    @each
    def _(p):
        for half in range(2):
            arrived(r_two + 3 * half + p, x_ref.at[0, 0, 0, 0])
            two_on(p, half).start()

    @each
    def _(p):
        arrived(r_two + 6 + p, x_ref.at[0, 0, 0])
        three_all(p, True)
        joined(p, 0).start()

    arrived(r_table + 1, first_c.at[pl.ds(0, 3)])
    for s in (1, 2, 3):
        table_wire(2, s).start()
    for load in loads[:4]:
        load.wait()
    arrived(r_join, half_of_quarter)
    gate_up(0)

    arrived(r_table + 2, table.at[pl.ds(0, 3)])
    lane = lax.broadcasted_iota(jnp.int32, (UNIT, 128), 1)
    row = lax.broadcasted_iota(jnp.int32, (UNIT, 128), 0)
    token = jnp.where(row < SHARE, row, row - SHARE) + place.expert * 16

    @pl.loop(0, 16)
    def _(yz):
        y, z = lax.div(yz, 4), lax.rem(yz, 4)
        rows = table[z, y]
        for x in range(4):
            pair = jnp.where(row < SHARE, rows[2 * x : 2 * x + 1], rows[2 * x + 1 : 2 * x + 2])
            at = (x, y, z)
            for p in range(PARTS):
                chosen = lane == token + p * SHARE
                value = jnp.sum(jnp.where(chosen, pair, 0.0), axis=1, keepdims=True)
                weight[p, at[(p + 2) % 3], at[(p + 1) % 3], at[p]] = jnp.broadcast_to(
                    value, (UNIT, 128)
                )

    for load in loads[4:]:
        load.wait()
    down(0)

    @each
    def _(p):
        for half in range(2):
            arrived(r_three + 3 * half + p, x_ref.at[0, 0, 0])
            for g in range(4):
                three_on(p, half, g).start()
            joined(p, 3 if half == 0 else 1, half).start()

    @each
    def _(p):
        arrived(r_three + 6 + p, x_ref.at[0, pl.ds(0, 2), 0])
        joined(p, 3, 1).start()
        joined(p, 1, 0).start()

    sent(s_two, x_ref.at[:, :, 0, 0])
    sent(s_two + 1, far1.at[0])
    sent(s_three, x_ref.at[:, :, 0])
    sent(s_join, half_of_quarter)
    free(3)
    arrived(r_join + 3, half_of_quarter)
    gate_up(3)
    merge(0)
    down(3)
    arrived(r_join + 1, half_of_quarter)
    gate_up(1)

    @each
    def _(p):
        for g in range(4):
            arrived(r_three + 9 + 3 * g + p, x_ref.at[0, 0, 0, pl.ds(0, 2)])
            for half in range(2):
                joined(p, 2, half, g).start()

    sent(s_three + 1, x_ref.at[:, 0, 0])
    sent(s_join + 3, half_of_quarter)
    free(1)
    sent(s_three + 2, x_ref.at[:, 0, 0])
    sent(s_join + 1, half_of_quarter)
    free(2)
    merge(3)
    down(1)
    arrived(r_join + 2, half_of_quarter)
    gate_up(2)
    merge(1)
    total(0)
    down(2)
    total(3)
    merge(2)
    total(1)

    def finish(d):
        @each
        def _(p):
            z3[d - 1, p] = chip_sum(p, d).astype(BF16)
            third(p, d).start()

    finish(3)
    finish(1)
    total(2)
    finish(2)

    @each
    def _(p):
        result = chip_sum(p, 0)
        arrived(r_third + p, got3.at[:, 0])
        for d in (3, 1, 2):
            result = result + got3[d - 1, p].astype(F32)
        o_ref[core, p] = result.astype(BF16)

    last.start()

    sent(s_deal, first.at[:, pl.ds(0, 7)])
    sent(s_table, first_c.at[pl.ds(0, 7)])
    sent(s_table + 1, first_c.at[pl.ds(0, 3)])
    sent(s_table + 2, table.at[pl.ds(0, 3)])
    sent(s_join + 2, half_of_quarter)
    sent(s_hand, x_ref.at[:, pl.ds(0, 2)])
    sent(s_ring, far1)
    sent(s_ring + 1, far1)
    sent(s_ring + 2, far1)
    sent(s_second, got2)
    sent(s_third, got3)
    last.wait_recv()
    for k in range(4):
        rows = []
        for p in range(PARTS):
            both = o_ref[k // 2, p].astype(F32)
            at = (k % 2) * UNIT
            rows.append(
                jnp.where(core == 0, both[at : at + SHARE], both[at + SHARE : at + 2 * SHARE])
            )
        out_ref[:, k * width : (k + 1) * width] = jnp.concatenate(rows, axis=0).astype(BF16)
    last.wait_send()


def on_device(tokens, routes, combine, gate_weight, up_weight, down_weight):
    model_width = tokens.shape[1]
    width = model_width // 4
    ff = gate_weight.shape[2]
    vmem = pl.BlockSpec(memory_space=pltpu.VMEM)
    hbm = pl.BlockSpec(memory_space=pl.ANY)

    def ring_buffer():
        return pltpu.VMEM((4, PARTS, 2, GROUP, width), BF16)

    return pl.pallas_call(
        kernel,
        out_shape=jax.ShapeDtypeStruct((ROWS, model_width), BF16),
        in_specs=[vmem, vmem, vmem, hbm, hbm, hbm],
        out_specs=vmem,
        scratch_shapes=[
            pltpu.VMEM((model_width, 2 * ff), BF16),
            pltpu.VMEM((4, ff, width), BF16),
            pltpu.VMEM((2, PARTS, 2 * SHARE, width), BF16),
            pltpu.VMEM((8, 128), F32),
            pltpu.VMEM((8, 128), F32),
            pltpu.VMEM((8, 128), jnp.int32),
            pltpu.VMEM((PARTS, 8, 2 * SHARE, width), BF16),
            pltpu.VMEM((8, 8, 128), F32),
            pltpu.VMEM((PARTS, 4, 4, 4, GROUP, width), BF16),
            pltpu.VMEM((PARTS, 4, 4, GROUP, width), BF16),
            pltpu.VMEM((PARTS * QUARTER, ff), BF16),
            pltpu.VMEM((4, 4, 8, 128), F32),
            pltpu.VMEM((PARTS, 4, 4, 4, UNIT, 128), F32),
            ring_buffer(),
            ring_buffer(),
            ring_buffer(),
            pltpu.VMEM((4, PARTS, 4, 2 * UNIT, width), BF16),
            pltpu.VMEM((4, PARTS, 3, 2 * UNIT, width), BF16),
            pltpu.VMEM((3, PARTS, 2 * UNIT, width), BF16),
            pltpu.VMEM((3, PARTS, 2 * UNIT, width), BF16),
            pltpu.VMEM((2, PARTS, 2 * UNIT, width), BF16),
            pltpu.SemaphoreType.DMA((8,)),
            pltpu.SemaphoreType.DMA((SENDS,)),
            pltpu.SemaphoreType.DMA((RECVS,)),
            pltpu.SemaphoreType.REGULAR((4,)),
        ],
        compiler_params=pltpu.CompilerParams(
            collective_id=0, has_side_effects=True, vmem_limit_bytes=62 * 2**20
        ),
    )(tokens, routes.T, combine.T, gate_weight[0], up_weight[0], down_weight[0])


def solution(mesh):
    placed = (
        P(("expert", "hidden"), None),
        P(("expert", "hidden"), None),
        P(("expert", "hidden"), None),
        P("expert", None, "hidden"),
        P("expert", None, "hidden"),
        P("expert", "hidden", None),
    )
    return jax.shard_map(
        on_device,
        mesh=mesh,
        in_specs=placed,
        out_specs=P(("expert", "hidden"), None),
        check_vma=False,
    )
```

time: 126 us -> 117 us (0.929)
  Pallas kernels: 121 us -> 116 us
  local copies, waits for them, and re-layouts: 3.93 us -> 1.62 us
  other arithmetic: 1.38 us -> 0 us
    pallas_call x1, Pallas kernels: 121 us -> 116 us  [on_device(): pl.pallas_call(kernel, out_shape=jax.ShapeDtypeStruct((ROWS, model_width)...]
    reshape x6 -> x0, local copies, waits for them, and re-layouts: 3.65 us -> none  [the longest x2 1.07 us: on_device(): tokens.reshape(PARTS, SHARE, 2, 2, width).transpose(2, 0, 3, 1, 4)]
    unnamed x0 -> x1, local copies, waits for them, and re-layouts: none -> 1.62 us
where the time goes in v3:
time: 117 us
  Pallas kernels  116 us (99%)
  local copies, waits for them, and re-layouts  1.62 us (1%)
    pallas_call x1, Pallas kernels, on_device(): pl.pallas_call(kernel, out_shape=jax.ShapeDtypeStruct((ROWS, model_width)...  116 us

profile of v3, /device:TPU:1, one launch (start us, length us, event | category | flops | bytes accessed | tf_op | source)
XLA Modules:
  0.0 117.2 jit_solution(1162860739858542538)
XLA Ops:
  0.0 115.6 %shard_map.64 = bf16[12,6144]{1,0:T(8,128)(2,1)} custom-call(bf16[12,6144]{1,0:T(8,128)(2,1)} %tok_ref.1, s32[2,12]{1,0:T(2,128)} %bitcast.8, f32[2,12]{1,0:T(2,128)} %bitcast.9, bf16[6144,512]{1,0:T(8,128)(2,1)} %bitcast.5, bf16[6144,512]{1,0:T(8,128)(2,1)} %bitcast.6, bf16[512,6144]{1,0:T(8,128)(2,1)} %bitcast.7), custom_call_target="tpu_custom_call" | custom-call | tf_op jit(solution)/shard_map/pallas_call | solution.py:531
  115.6 1.6 %copy.8 = bf16[12,6144]{1,0:T(8,128)(2,1)} copy(bf16[12,6144]{1,0:T(8,128)(2,1)} %shard_map.64) | data formatting | bytes 294912

commit v4 on v3

--- a/solution.py
+++ b/solution.py
@@ -269,8 +269,7 @@
     last = wire(s_last, r_last, o_ref.at[core], o_ref.at[core], sibling)
 
     def gate_up(d):
-        @pl.loop(0, 2)
-        def _(n):
+        for n in range(2):
             rows = jnp.concatenate(
                 [
                     jnp.concatenate(
@@ -280,11 +279,11 @@
                 ],
                 axis=0,
             )
-            cols = pl.ds(pl.multiple_of(n * ff, ff), ff)
+            cols = pl.ds(n * ff, ff)
             result = jnp.dot(rows, w_ref[:, cols], preferred_element_type=F32)
             gate, up = result[:, :block], result[:, block:]
             hidden = gate / (1.0 + jnp.exp(-gate)) * up
-            h_ref[:, pl.ds(pl.multiple_of(n * block, block), block)] = hidden.astype(BF16)
+            h_ref[:, pl.ds(n * block, block)] = hidden.astype(BF16)
 
     def down(d):
         def scaled(k):
@@ -372,7 +371,6 @@
             x_ref[p, 2 * core + half, 0, 0] = jnp.concatenate(halves[half], axis=0).astype(BF16)
         for half, step in ((0, 1), (1, 3), (1, 1), (0, 3)):
             two(p, half, step).start()
-        three_all(p, False)
 
     arrived(r_table, first_c.at[pl.ds(0, 7)])
     row8 = lax.broadcasted_iota(jnp.int32, (8, 128), 0)
@@ -385,6 +383,7 @@
         for half in range(2):
             arrived(r_two + 3 * half + p, x_ref.at[0, 0, 0, 0])
             two_on(p, half).start()
+        three_all(p, False)
 
     @each
     def _(p):
@@ -444,14 +443,11 @@
     free(3)
     arrived(r_join + 3, half_of_quarter)
     gate_up(3)
-    merge(0)
     down(3)
-    arrived(r_join + 1, half_of_quarter)
-    gate_up(1)
-
-    @each
-    def _(p):
-        for g in range(4):
+
+    for g in range(4):
+        @each
+        def _(p):
             arrived(r_three + 9 + 3 * g + p, x_ref.at[0, 0, 0, pl.ds(0, 2)])
             for half in range(2):
                 joined(p, 2, half, g).start()
@@ -459,15 +455,18 @@
     sent(s_three + 1, x_ref.at[:, 0, 0])
     sent(s_join + 3, half_of_quarter)
     free(1)
+    arrived(r_join + 1, half_of_quarter)
+    gate_up(1)
+    merge(0)
     sent(s_three + 2, x_ref.at[:, 0, 0])
     sent(s_join + 1, half_of_quarter)
     free(2)
+    down(1)
     merge(3)
-    down(1)
     arrived(r_join + 2, half_of_quarter)
     gate_up(2)
+    total(0)
     merge(1)
-    total(0)
     down(2)
     total(3)
     merge(2)

time: 117 us -> 113 us (0.966)
  Pallas kernels: 116 us -> 111 us
    pallas_call x1, Pallas kernels: 116 us -> 111 us  [on_device(): pl.pallas_call(kernel, out_shape=jax.ShapeDtypeStruct((ROWS, model_width)...]
where the time goes in v4:
time: 113 us; the launch traced here: 112 us
  Pallas kernels  111 us (98%)
  local copies, waits for them, and re-layouts  1.62 us (1%)
    pallas_call x1, Pallas kernels, on_device(): pl.pallas_call(kernel, out_shape=jax.ShapeDtypeStruct((ROWS, model_width)...  111 us

profile of v4, /device:TPU:1, one launch (start us, length us, event | category | flops | bytes accessed | tf_op | source)
XLA Modules:
  0.0 112.4 jit_solution(2662478319918573094)
XLA Ops:
  0.0 110.8 %shard_map.64 = bf16[12,6144]{1,0:T(8,128)(2,1)} custom-call(bf16[12,6144]{1,0:T(8,128)(2,1)} %tok_ref.1, s32[2,12]{1,0:T(2,128)} %bitcast.8, f32[2,12]{1,0:T(2,128)} %bitcast.9, bf16[6144,512]{1,0:T(8,128)(2,1)} %bitcast.5, bf16[6144,512]{1,0:T(8,128)(2,1)} %bitcast.6, bf16[512,6144]{1,0:T(8,128)(2,1)} %bitcast.7), custom_call_target="tpu_custom_call" | custom-call | tf_op jit(solution)/shard_map/pallas_call | solution.py:530
  110.8 1.6 %copy.8 = bf16[12,6144]{1,0:T(8,128)(2,1)} copy(bf16[12,6144]{1,0:T(8,128)(2,1)} %shard_map.64) | data formatting | bytes 294912

commit v5 on v4

--- a/solution.py
+++ b/solution.py
@@ -87,7 +87,7 @@
 def kernel(
     tok_ref, route_ref, comb_ref, gate_ref, up_ref, down_ref, out_ref,
     w_ref, wd_ref, t_ref, c_ref, pad_c, pad_r, first, first_c, x_ref, y_ref, h_ref, table, weight,
-    far1, plain1, merged1, z2, got2, z3, got3, o_ref,
+    far1, plain1, merged1, z2, got2, z3, got3,
     load_sem, send_sem, recv_sem, credit,
 ):
     place = Place()
@@ -252,7 +252,6 @@
 
     s_second, r_second = sends.take(1), recvs.take(12)
     s_third, r_third = sends.take(1), recvs.take(3)
-    s_last, r_last = sends.take(1), recvs.take(1)
     assert sends.count <= SENDS and recvs.count <= RECVS
 
     def second(p, d, s):
@@ -261,12 +260,11 @@
             place.along(p, 0, s),
         )
 
-    def third(p, d):
-        return wire(
-            s_third, r_third + p, z3.at[d - 1, p], got3.at[d - 1, p], place.along(p, 2, d)
-        )
-
-    last = wire(s_last, r_last, o_ref.at[core], o_ref.at[core], sibling)
+    def third(p, d, o):
+        to = 1 - core if o else core
+        return wire(
+            s_third, r_third + p, z3.at[d, p, to], got3.at[o, d, p], place.along(p, 2, d, o)
+        )
 
     def gate_up(d):
         for n in range(2):
@@ -475,23 +473,22 @@
     def finish(d):
         @each
         def _(p):
-            z3[d - 1, p] = chip_sum(p, d).astype(BF16)
-            third(p, d).start()
-
+            result = chip_sum(p, d)
+            for to in range(2):
+                rows = [
+                    result[half * UNIT + to * SHARE : half * UNIT + (to + 1) * SHARE]
+                    for half in range(2)
+                ]
+                z3[d, p, to] = jnp.concatenate(rows, axis=0).astype(BF16)
+            if d:
+                third(p, d, 0).start()
+            third(p, d, 1).start()
+
+    finish(0)
     finish(3)
     finish(1)
     total(2)
     finish(2)
-
-    @each
-    def _(p):
-        result = chip_sum(p, 0)
-        arrived(r_third + p, got3.at[:, 0])
-        for d in (3, 1, 2):
-            result = result + got3[d - 1, p].astype(F32)
-        o_ref[core, p] = result.astype(BF16)
-
-    last.start()
 
     sent(s_deal, first.at[:, pl.ds(0, 7)])
     sent(s_table, first_c.at[pl.ds(0, 7)])
@@ -503,18 +500,25 @@
     sent(s_ring + 1, far1)
     sent(s_ring + 2, far1)
     sent(s_second, got2)
-    sent(s_third, got3)
-    last.wait_recv()
-    for k in range(4):
-        rows = []
-        for p in range(PARTS):
-            both = o_ref[k // 2, p].astype(F32)
-            at = (k % 2) * UNIT
-            rows.append(
-                jnp.where(core == 0, both[at : at + SHARE], both[at + SHARE : at + 2 * SHARE])
-            )
-        out_ref[:, k * width : (k + 1) * width] = jnp.concatenate(rows, axis=0).astype(BF16)
-    last.wait_send()
+    columns = ([], [])
+    for p in range(PARTS):
+        arrived(r_third + p, first.at[p, pl.ds(0, 7)])
+        for o in range(2):
+            part = z3[0, p, core].astype(F32) if o == 0 else got3[1, 0, p].astype(F32)
+            for d in (3, 1, 2):
+                part = part + got3[o, d, p].astype(F32)
+            columns[o].append(part)
+    for half in range(2):
+        same, other = [
+            jnp.concatenate([c[half * SHARE : (half + 1) * SHARE] for c in columns[o]], axis=0)
+            for o in range(2)
+        ]
+        for k, value in enumerate(
+            (jnp.where(core == 0, same, other), jnp.where(core == 0, other, same))
+        ):
+            at = (2 * k + half) * width
+            out_ref[:, at : at + width] = value.astype(BF16)
+    sent(s_third, first.at[:, pl.ds(0, 7)])
 
 
 def on_device(tokens, routes, combine, gate_weight, up_weight, down_weight):
@@ -551,9 +555,8 @@
             ring_buffer(),
             pltpu.VMEM((4, PARTS, 4, 2 * UNIT, width), BF16),
             pltpu.VMEM((4, PARTS, 3, 2 * UNIT, width), BF16),
-            pltpu.VMEM((3, PARTS, 2 * UNIT, width), BF16),
-            pltpu.VMEM((3, PARTS, 2 * UNIT, width), BF16),
-            pltpu.VMEM((2, PARTS, 2 * UNIT, width), BF16),
+            pltpu.VMEM((4, PARTS, 2, 2 * SHARE, width), BF16),
+            pltpu.VMEM((2, 4, PARTS, 2 * SHARE, width), BF16),
             pltpu.SemaphoreType.DMA((8,)),
             pltpu.SemaphoreType.DMA((SENDS,)),
             pltpu.SemaphoreType.DMA((RECVS,)),

time: 113 us -> 111 us (0.982)
  Pallas kernels: 111 us -> 109 us
    pallas_call x1, Pallas kernels: 111 us -> 109 us  [on_device(): pl.pallas_call(kernel, out_shape=jax.ShapeDtypeStruct((ROWS, model_width)...]
where the time goes in v5:
time: 111 us
  Pallas kernels  109 us (98%)
  local copies, waits for them, and re-layouts  1.62 us (1%)
    pallas_call x1, Pallas kernels, on_device(): pl.pallas_call(kernel, out_shape=jax.ShapeDtypeStruct((ROWS, model_width)...  109 us

profile of v5, /device:TPU:1, one launch (start us, length us, event | category | flops | bytes accessed | tf_op | source)
XLA Modules:
  0.0 111.0 jit_solution(6675578806557246515)
XLA Ops:
  0.0 109.4 %shard_map.64 = bf16[12,6144]{1,0:T(8,128)(2,1)} custom-call(bf16[12,6144]{1,0:T(8,128)(2,1)} %tok_ref.1, s32[2,12]{1,0:T(2,128)} %bitcast.8, f32[2,12]{1,0:T(2,128)} %bitcast.9, bf16[6144,512]{1,0:T(8,128)(2,1)} %bitcast.5, bf16[6144,512]{1,0:T(8,128)(2,1)} %bitcast.6, bf16[512,6144]{1,0:T(8,128)(2,1)} %bitcast.7), custom_call_target="tpu_custom_call" | custom-call | tf_op jit(solution)/shard_map/pallas_call | solution.py:534
  109.4 1.6 %copy.8 = bf16[12,6144]{1,0:T(8,128)(2,1)} copy(bf16[12,6144]{1,0:T(8,128)(2,1)} %shard_map.64) | data formatting | bytes 294912

commit v6 on v5

--- a/solution.py
+++ b/solution.py
@@ -463,9 +463,9 @@
     merge(3)
     arrived(r_join + 2, half_of_quarter)
     gate_up(2)
-    total(0)
     merge(1)
     down(2)
+    total(0)
     total(3)
     merge(2)
     total(1)

time: 111 us -> 113 us (1.018)
  Pallas kernels: 109 us -> 111 us
    pallas_call x1, Pallas kernels: 109 us -> 111 us  [on_device(): pl.pallas_call(kernel, out_shape=jax.ShapeDtypeStruct((ROWS, model_width)...]
where the time goes in v6:
time: 113 us; the launch traced here: 112 us
  Pallas kernels  111 us (98%)
  local copies, waits for them, and re-layouts  1.62 us (1%)
    pallas_call x1, Pallas kernels, on_device(): pl.pallas_call(kernel, out_shape=jax.ShapeDtypeStruct((ROWS, model_width)...  111 us

profile of v6, /device:TPU:1, one launch (start us, length us, event | category | flops | bytes accessed | tf_op | source)
XLA Modules:
  0.0 112.5 jit_solution(9351843208949373403)
XLA Ops:
  0.0 110.8 %shard_map.64 = bf16[12,6144]{1,0:T(8,128)(2,1)} custom-call(bf16[12,6144]{1,0:T(8,128)(2,1)} %tok_ref.1, s32[2,12]{1,0:T(2,128)} %bitcast.8, f32[2,12]{1,0:T(2,128)} %bitcast.9, bf16[6144,512]{1,0:T(8,128)(2,1)} %bitcast.5, bf16[6144,512]{1,0:T(8,128)(2,1)} %bitcast.6, bf16[512,6144]{1,0:T(8,128)(2,1)} %bitcast.7), custom_call_target="tpu_custom_call" | custom-call | tf_op jit(solution)/shard_map/pallas_call | solution.py:534
  110.8 1.6 %copy.8 = bf16[12,6144]{1,0:T(8,128)(2,1)} copy(bf16[12,6144]{1,0:T(8,128)(2,1)} %shard_map.64) | data formatting | bytes 294912
